TPU v7x, 32 devices: a whole 2x2x4 slice. The times are simulated.
32 devices in a mesh: seq: 8 (over z, y), head: 4 (over x, core).
Axes of the slice: x: 2, y: 2, z: 4, core: 2. Of those that a mesh axis runs over, the one named last changes fastest.
Arguments:
- tokens: bfloat16 [4096, 4096], P('seq'), may hold values from -6 to 6
- w_query: bfloat16 [4096, 4096], P(None, 'head'), may hold values from -0.09375 to 0.09375
- w_key: bfloat16 [4096, 4096], P(None, 'head'), may hold values from -0.09375 to 0.09375
- w_value: bfloat16 [4096, 4096], P(None, 'head'), may hold values from -0.09375 to 0.09375
- w_out: bfloat16 [4096, 4096], P('head'), may hold values from -0.125 to 0.125
- norm_gain: float32 [4096], P('head'), may hold values from 0.1 to 1.9
- level_weights: float32 [21, 32, 4096], P(None, 'head', 'seq'), may hold values from 0.00024414062 to 4, as said below
- prior_states: float32 [4, 32, 128, 128], P(None, 'head'), may hold values from -96 to 96
Outputs:
- layer_out: bfloat16 [4096, 4096], P('seq', 'head')
Inputs may be any that keep to these rules, and one draw needn't show every extreme that they name: `level_weights`: positive.
All inputs are finite; a program needn't handle non-finite values.
Results may differ from a plain program's by a relative error of at most 0.022.
Values may be sent and summed in bfloat16 or wider, within the bound.
No kernel may reach another device: no remote copies, remote signals or barrier semaphores. Data moves between devices by JAX's collectives and lax.ppermute only.
A program may use at most 128 MiB of HBM per device.

v0:
```python
import functools

import jax
import jax.numpy as jnp
from jax import lax
from jax.experimental import pallas as pl
from jax.experimental.pallas import tpu as pltpu
from jax.sharding import PartitionSpec as P

eps = 1e-06
TILE = 128
MIB = 1024 * 1024
f32, bf16 = jnp.float32, jnp.bfloat16
HBM = pl.BlockSpec(memory_space=pltpu.HBM)
VMEM = pl.BlockSpec(memory_space=pltpu.VMEM)
SMEM = pl.BlockSpec(memory_space=pltpu.SMEM)
ANY = pl.BlockSpec(memory_space=pl.ANY)


def mm(a, b):
    return jnp.dot(a, b, preferred_element_type=f32)


def params(mib):
    return pltpu.CompilerParams(vmem_limit_bytes=mib * MIB)


def cost(flops, size):
    return pl.CostEstimate(flops=int(flops) // 100, bytes_accessed=int(size) // 100, transcendentals=0)


FAR_APART = pl.CostEstimate(flops=4 * 10**10, bytes_accessed=10**8, transcendentals=0)


def in_hbm(x):
    return pltpu.with_memory_space_constraint(x, pltpu.HBM)


def starts(copies):
    for copy in copies:
        copy.start()


def keys_values_body(
    width, x_hbm, wk_hbm, wv_hbm, wq_hbm, x, wq, k_ref, vt_ref, keep_ref, give_ref, wk, wv, k_acc, v_acc, s, sem
):
    rows, depth = x.shape
    size = wk.shape[1]
    cuts = sem.shape[1]
    cut = depth // cuts
    at = [pl.ds(c * cut, cut) for c in range(cuts)]
    x_in = [pltpu.make_async_copy(x_hbm.at[:, a], x.at[:, a], sem.at[0, c]) for c, a in enumerate(at)]
    v_in = [pltpu.make_async_copy(wv_hbm.at[a], wv.at[a], sem.at[1, c]) for c, a in enumerate(at)]
    k_in = [pltpu.make_async_copy(wk_hbm.at[a], wk.at[a], sem.at[2, c]) for c, a in enumerate(at)]
    q_in = [pltpu.make_async_copy(wq_hbm.at[a], wq.at[a], sem.at[3, c]) for c, a in enumerate(at)]
    for c in range(cuts):
        starts((x_in[c], v_in[c]))
    starts(k_in)
    starts(q_in)
    heads = size // width
    half = heads // 2
    own = [slice(h * width, (h + 1) * width) for h in range(heads)]
    for c, a in enumerate(at):
        x_in[c].wait()
        v_in[c].wait()
        term = mm(x[:, a], wv[a, :])
        v_acc[...] = term if c == 0 else v_acc[...] + term
    for c, a in enumerate(at):
        k_in[c].wait()
        term = mm(x[:, a], wk[a, :])
        k_acc[...] = term if c == 0 else k_acc[...] + term
        for h in range(c * heads // cuts, (c + 1) * heads // cuts):
            vt_ref[own[h], :] = v_acc[:, own[h]].T.astype(bf16)
    for h in range(heads):
        raw = k_acc[:, own[h]]
        key = (raw * lax.rsqrt(jnp.sum(raw * raw, axis=-1, keepdims=True) + eps)).astype(bf16)
        k_ref[:, own[h]] = key
        s[h] = mm(vt_ref[own[h], :], key).astype(bf16)
    first = (lax.axis_index("seq") & 1) * half
    for h in range(half):
        keep_ref[h] = s[first + h]
        give_ref[h] = s[half - first + h]
    for copy in q_in:
        copy.wait()


def keys_values(tokens, w_key, w_value, w_query, width):
    rows, depth = tokens.shape
    size = w_key.shape[1]
    heads = size // width
    cuts = 8
    part = pltpu.VMEM((heads // 2, width, width), bf16)
    return pl.pallas_call(
        functools.partial(keys_values_body, width),
        in_specs=[HBM] * 4,
        out_specs=[VMEM] * 6,
        out_shape=[
            pltpu.VMEM((rows, depth), bf16),
            pltpu.VMEM((depth, size), bf16),
            pltpu.VMEM((rows, size), bf16),
            pltpu.VMEM((size, rows), bf16),
            part,
            part,
        ],
        scratch_shapes=[
            pltpu.VMEM((depth, size), bf16),
            pltpu.VMEM((depth, size), bf16),
            pltpu.VMEM((rows, size), f32),
            pltpu.VMEM((rows, size), f32),
            pltpu.VMEM((heads, width, width), bf16),
            pltpu.SemaphoreType.DMA((4, cuts)),
        ],
        compiler_params=params(30),
        cost_estimate=cost(4 * rows * depth * size, 2 * (rows * depth + 2 * depth * size)),
        name="keys_values",
    )(in_hbm(tokens), in_hbm(w_key), in_hbm(w_value), in_hbm(w_query))


def attend(qt, k, vt, lam, prior):
    width, rows = qt.shape
    shift = rows.bit_length() - 1
    low = TILE.bit_length() - 1
    levels, priors = lam.shape[0], len(prior)
    product = mm(jnp.concatenate([p.astype(bf16).T for p in prior], axis=0), qt)
    total = lam[levels - priors : levels - priors + 1] * product[:width]
    for p in range(1, priors):
        lv = levels - priors + p
        total = total + lam[lv : lv + 1] * product[p * width : (p + 1) * width]
    t_at = lax.broadcasted_iota(jnp.int32, (8, rows), 1) & 7
    s_at = lax.broadcasted_iota(jnp.int32, (8, rows), 0)
    near = jnp.zeros((8, rows), f32)
    for lv in range(4):
        picked = (t_at ^ s_at) >= (1 << lv >> 1)
        near = jnp.where(picked, lam[lv : lv + 1], near)
    near = jnp.where(s_at <= t_at, near, 0.0)
    groups = TILE // 8
    t_group = (lax.broadcasted_iota(jnp.int32, (groups, rows), 1) & (TILE - 1)) >> 3
    s_group = lax.broadcasted_iota(jnp.int32, (groups, rows), 0)
    wide = jnp.zeros((groups, rows), f32)
    for lv in range(4, low + 1):
        picked = (t_group ^ s_group) >= (1 << (lv - 4))
        wide = jnp.where(picked, lam[lv : lv + 1], wide)
    wide = jnp.where(s_group < t_group, wide, 0.0)
    lane_group = (lax.broadcasted_iota(jnp.int32, (8, TILE), 1)) >> 3
    pieces = []
    for i in range(rows // TILE):
        here = slice(i * TILE, (i + 1) * TILE)
        scores = mm(k[here], qt[:, here])
        mixing = []
        for g in range(groups):
            weight = jnp.where(lane_group == g, near[:, here], wide[g : g + 1, here])
            mixing.append(weight * scores[g * 8 : g * 8 + 8])
        mixing = jnp.concatenate(mixing, axis=0).astype(bf16)
        pieces.append(total[:, here] + mm(vt[:, here], mixing))
    for bit in range(low, shift):
        half = 1 << bit
        for start in range(half, rows, 2 * half):
            past = slice(start - half, start)
            here = slice(start, start + half)
            state = mm(vt[:, past], k[past]).astype(bf16)
            found = lam[1 + bit : 2 + bit, here] * mm(state, qt[:, here])
            for n in range(half // TILE):
                i = start // TILE + n
                pieces[i] = pieces[i] + found[:, n * TILE : (n + 1) * TILE]
    return pieces


def attend_into(acc_ref, at, head, h, width, qt, k_ref, vt_ref, lam_ref, prior_ref):
    own = slice(h * width, (h + 1) * width)
    prior = [prior_ref[p, h] for p in range(prior_ref.shape[0])]
    pieces = attend(qt, k_ref[:, own], vt_ref[own, :], lam_ref[:, head, :], prior)
    for i, piece in enumerate(pieces):
        acc_ref[i, at * width : (at + 1) * width, :] = piece


def whole(qt_ref, at):
    return jnp.concatenate([qt_ref[i, at, :] for i in range(qt_ref.shape[0])], axis=1)


def queries_body(width, part, flip, count, x, wq, after, w_hbm, *refs):
    sources, qt_ref, w_ref, targets, sem = refs[:count], refs[count], refs[count + 1], refs[count + 2 : -1], refs[-1]
    copies = [pltpu.make_async_copy(a, b, sem.at[n]) for n, (a, b) in enumerate(zip(sources, targets))]
    chips, _, columns = w_ref.shape
    group = lax.axis_index("head") ^ flip
    for d in range(chips):
        base = pl.multiple_of(lax.rem(group + 2 * d, 2 * chips) * columns, 128)
        copies.append(pltpu.make_async_copy(w_hbm.at[:, pl.ds(base, columns)], w_ref.at[d], sem.at[count + d]))
    starts(copies)
    rows = x.shape[0]
    size = qt_ref.shape[1]
    step = min(256, size)
    for first in range(0, size, step):
        raw_step = mm(x[...], wq[:, part * size + first : part * size + first + step])
        for h in range(step // width):
            raw = raw_step[:, h * width : (h + 1) * width].T
            qt = (raw * lax.rsqrt(jnp.sum(raw * raw, axis=0, keepdims=True) + eps)).astype(bf16)
            own = slice(first + h * width, first + (h + 1) * width)
            for i in range(rows // TILE):
                qt_ref[i, own, :] = qt[:, i * TILE : (i + 1) * TILE]
    for copy in copies:
        copy.wait()


def queries(tokens, w_query, after, w_out, flip, chips, width, part, fetch=()):
    rows, depth = tokens.shape
    size = w_query.shape[1] // 2
    columns = w_out.shape[1] // (2 * chips)
    return pl.pallas_call(
        functools.partial(queries_body, width, part, flip, len(fetch)),
        in_specs=[VMEM, VMEM, ANY, HBM] + [HBM] * len(fetch),
        out_specs=[VMEM] * (2 + len(fetch)),
        out_shape=[pltpu.VMEM((rows // TILE, size, TILE), bf16), pltpu.VMEM((chips, w_out.shape[0], columns), bf16)]
        + [pltpu.VMEM(a.shape, a.dtype) for a in fetch],
        scratch_shapes=[pltpu.SemaphoreType.DMA((len(fetch) + chips,))],
        compiler_params=params(16),
        cost_estimate=cost(2 * rows * depth * size, 2 * (rows * depth + depth * size)),
        name="queries",
    )(tokens, w_query, after, in_hbm(w_out), *[in_hbm(a) for a in fetch])


def attention_body(width, halves, k_ref, vt_ref, lam_ref, prior_ref, after, *refs):
    qt_refs, acc_ref = refs[:halves], refs[halves]
    heads = prior_ref.shape[1]
    per = heads // halves
    for h in range(heads):
        qt = whole(qt_refs[h // per], slice(h % per * width, (h % per + 1) * width))
        attend_into(acc_ref, h, h, h, width, qt, k_ref, vt_ref, lam_ref, prior_ref)


def attention(queries_t, keys, values_t, level_weights, prior_states, after, width):
    tiles, _, take = queries_t[0].shape
    total = keys.shape[1]
    return pl.pallas_call(
        functools.partial(attention_body, width, len(queries_t)),
        in_specs=[VMEM] * 4 + [ANY] + [VMEM] * len(queries_t),
        out_specs=VMEM,
        out_shape=pltpu.VMEM((tiles, total, take), f32),
        compiler_params=params(16),
        cost_estimate=cost(12 * tiles * take * width * total, 8 * tiles * take * total),
        name="attention",
    )(keys, values_t, level_weights, prior_states, after, *queries_t)


def far_body(width, first_level, halves, nbits, first, number, after, *refs):
    qt_refs = refs[:halves]
    acc_ref = refs[halves]
    state_refs = refs[halves + 1 : halves + 1 + 2 * nbits]
    lam_ref, gain_ref, out_ref = refs[halves + 1 + 2 * nbits :]
    heads = lam_ref.shape[1]
    half = heads // 2
    per = heads // halves
    mine = lax.axis_index("seq")
    odd = (mine & 1) > 0
    for head in range(heads):
        own = slice(head * width, (head + 1) * width)
        states = []
        for j in range(nbits):
            kept, swapped = state_refs[2 * j][head % half], state_refs[2 * j + 1][head % half]
            if j == 0:
                states.append(kept if head >= half else swapped)
            else:
                states.append(jnp.where(odd, kept, swapped) if head >= half else jnp.where(odd, swapped, kept))
        states = jnp.concatenate(states, axis=0)
        for i in range(number):
            tile = first + i
            qt = qt_refs[head // per][tile, head % per * width : (head % per + 1) * width, :]
            product = mm(states, qt)
            total = acc_ref[tile, own, :]
            for j in range(nbits):
                lam = lam_ref[first_level + j, head : head + 1, tile * TILE : (tile + 1) * TILE]
                lam = jnp.where(((mine >> j) & 1) > 0, lam, 0.0)
                total = total + lam * product[j * width : (j + 1) * width]
            scale = lax.rsqrt(jnp.mean(total * total, axis=0, keepdims=True) + eps)
            out_ref[i * TILE : (i + 1) * TILE, own] = ((total * scale).T * gain_ref[:, own]).astype(bf16)


def far_part(after, queries_t, acc, states, level_weights, gain, width, first, number):
    levels, heads, rows = level_weights.shape
    total = heads * width
    halves = len(queries_t)
    return pl.pallas_call(
        functools.partial(far_body, width, rows.bit_length(), halves, len(states) // 2, first, number),
        in_specs=[ANY] + [VMEM] * (halves + 3 + len(states)),
        out_specs=VMEM,
        out_shape=pltpu.VMEM((number * TILE, total), bf16),
        compiler_params=params(16),
        cost_estimate=cost(8 * rows * width * total, 8 * rows * total),
        name="far_part",
    )(after, *queries_t, acc, *states, level_weights, gain)


def project_body(d, count, after, w, w_twin, *refs):
    mine, twins, out_ref = refs[:count], refs[count : 2 * count], refs[2 * count]
    columns = w.shape[2]
    step = min(256, columns)
    for first in range(0, columns, step):
        here = slice(first, first + step)
        row = 0
        for a, b in zip(mine, twins):
            take = a.shape[0]
            total = mm(a[...], w[d, :, here]) + mm(b[...], w_twin[d, :, here])
            out_ref[row : row + take, here] = total.astype(out_ref.dtype)
            row += take


def project(after, w, w_twin, mine, twins, kind, d, estimate=None):
    _, depth, columns = w.shape
    take = sum(a.shape[0] for a in mine)
    return pl.pallas_call(
        functools.partial(project_body, d, len(mine)),
        in_specs=[ANY, VMEM, VMEM] + [VMEM] * (2 * len(mine)),
        out_specs=VMEM,
        out_shape=pltpu.VMEM((take, columns), kind),
        compiler_params=params(16),
        cost_estimate=estimate or cost(4 * take * depth * columns, 4 * depth * columns),
        name="project",
    )(after, w, w_twin, *mine, *twins)


def finish_body(count, out_in, own_ref, *refs):
    out_ref = refs[-1]
    total = own_ref[...]
    for ref in refs[:count]:
        total = total + ref[...].astype(f32)
    out_ref[...] = total.astype(bf16)


def finish(out, own, terms, first):
    rows, columns = own.shape
    place = lambda i: (first // TILE + i, 0)
    return pl.pallas_call(
        functools.partial(finish_body, len(terms)),
        grid=(terms[0].shape[0] // TILE,),
        in_specs=[ANY, pl.BlockSpec((TILE, columns), place)]
        + [pl.BlockSpec((TILE, columns), lambda i: (i, 0))] * len(terms),
        out_specs=pl.BlockSpec((TILE, columns), place),
        out_shape=jax.ShapeDtypeStruct((rows, columns), bf16),
        input_output_aliases={0: 0} if first else {},
        compiler_params=params(16),
        cost_estimate=FAR_APART,
        name="finish",
    )(out, own, *terms)


def per_device(tokens, w_query, w_key, w_value, w_out, norm_gain, level_weights, prior_states):
    levels, heads, rows = level_weights.shape
    width = prior_states.shape[-1]
    count = lax.axis_size("seq")
    nbits = count.bit_length() - 1
    groups = lax.axis_size("head")
    chips = groups // 2
    twin = [(i, i ^ 1) for i in range(groups)]
    gain = norm_gain.reshape(1, heads * width)

    def send(state, j):
        return lax.ppermute(state, "seq", [(r, r ^ (1 << j)) for r in range(count)])

    def merge(state, got):
        return (state.astype(f32) + got.astype(f32)).astype(bf16)

    def not_before(value, done):
        return lax.optimization_barrier((value, done))[0]

    tokens, w_query, keys, values_t, keep, give = keys_values(tokens, w_key, w_value, w_query, width)
    got = send(give, 0)
    q_a, w_give, level_weights, prior_states = queries(
        tokens, w_query, keep, w_out, 1, chips, width, 0, (level_weights, prior_states)
    )
    got = not_before(got, q_a)
    running = merge(keep, got)
    states = [got]
    for j in range(1, nbits):
        got = send(running, j)
        if j == 1:
            w_twin = lax.ppermute(not_before(w_give, running), "head", twin)
            states.append(send(not_before(keep, running), 0))
            done, w = queries(tokens, w_query, running, w_out, 0, chips, width, 1)
            queries_t = [q_a, done]
        elif j == nbits - 1:
            done = acc = attention(queries_t, keys, values_t, level_weights, prior_states, running, width)
        got = not_before(got, done)
        if j < nbits - 1:
            running = merge(running, got)
        states += [got, send(got, 0)]

    first = far_part(acc, queries_t, acc, states, level_weights, gain, width, 0, 1)
    first_twin = lax.ppermute(first, "head", twin)
    rest = far_part(first, queries_t, acc, states, level_weights, gain, width, 1, rows // TILE - 1)
    rest_twin = lax.ppermute(rest, "head", twin)
    after = rest
    received = []
    for mine, other, estimate in ((first, first_twin, FAR_APART), (rest, rest_twin, None)):
        terms = []
        for d in range(1, chips):
            after = project(after, w, w_twin, [mine], [other], bf16, d, estimate)
            terms.append(lax.ppermute(after, "head", [(i, (i + 2 * d) % groups) for i in range(groups)]))
        received.append(terms)
    own = project(after, w, w_twin, [first, rest], [first_twin, rest_twin], f32, 0)
    out = finish(gain, own, received[0], 0)
    return finish(out, own, received[1], TILE)


def solution(mesh):
    placed = (
        P("seq", None),
        P(None, "head"),
        P(None, "head"),
        P(None, "head"),
        P("head", None),
        P("head"),
        P(None, "head", "seq"),
        P(None, "head", None, None),
    )
    return jax.shard_map(
        per_device, mesh=mesh, in_specs=placed, out_specs=P("seq", "head"), check_vma=False
    )
```

profile of v0, /device:TPU:0, one launch (start us, length us, event | category | flops | bytes accessed | tf_op | source)
XLA Modules:
  0.0 69.4 jit_solution(11616848561043806266)
XLA Ops:
  0.0 12.0 %keys_values.1 = (bf16[512,4096]{1,0:T(8,128)(2,1)S(1)}, bf16[4096,1024]{1,0:T(8,128)(2,1)S(1)}, bf16[512,1024]{1,0:T(8,128)(2,1)S(1)}, bf16[1024,512]{1,0:T(8,1...) custom-call(bf16[512,4096]{1,0:T(8,128)(2,1)} %x_hbm.1, bf16[4096,1024]{1,0:T(8,128)(2,1)} %wk_hbm.1, ...), custom_call_target="tpu_custom_call" | custom-call | flops 85899344 | bytes 209715 | tf_op jit(solution)/shard_map/keys_values/pallas_call | solution.py:93
  12.0 3.0 %collective-permute-start = (bf16[4,128,128]{2,1,0:T(8,128)(2,1)S(1)}, bf16[4,128,128]{2,1,0:T(8,128)(2,1)S(1)}, u32[]{:S(2)}, u32[]{:S(2)}) collective-permute-start(bf16[4,128,128]{2,1,0:T(8,128)(2,1)S(1)} %get-tuple-element.29), channel_id=1, source_target_pairs={{0,4},{4,0},{8,12},{12,8},{16,20},{20,16},{24,28},{28,24},{1,5},{5... | collective-permute-start | bytes 393224 | tf_op jit(solution)/shard_map/ppermute | solution.py:356
  15.0 4.4 %queries.2 = (bf16[4,512,128]{2,1,0:T(8,128)(2,1)S(1)}, bf16[2,1024,1024]{2,1,0:T(8,128)(2,1)S(1)}, f32[21,8,512]{2,1,0:T(8,128)S(1)}, f32[4,8,128,128]{3,2,1,0:T(8,128)S(1)}) custom-call(bf16[512,4096]{1,0:T(8,128)(2,1)S(1)} %get-tuple-element.24.x, bf16[4096,1024]{1,0:T(8,128)(2,1)S(1)} %get-tuple-element.25.wq, ...), custom_call_target="tpu_custom_call" | custom-call | flops 21474836 | bytes 83886 | tf_op jit(solution)/shard_map/queries/pallas_call | solution.py:208
  19.5 1.6 %collective-permute-start.1 = (bf16[4,128,128]{2,1,0:T(8,128)(2,1)S(1)}, bf16[4,128,128]{2,1,0:T(8,128)(2,1)S(1)}, u32[]{:S(2)}, u32[]{:S(2)}) collective-permute-start(bf16[4,128,128]{2,1,0:T(8,128)(2,1)S(1)} %add_convert_fusion.1.after), channel_id=1, source_target_pairs={{0,8},{4,12},{8,0},{12,4},{16,24},{20,28},{24,16},{28,20},{1,9},{5... | collective-permute-start | bytes 393224 | tf_op jit(solution)/shard_map/ppermute | solution.py:356
  21.2 4.2 %queries.3 = (bf16[4,512,128]{2,1,0:T(8,128)(2,1)S(1)}, bf16[2,1024,1024]{2,1,0:T(8,128)(2,1)S(1)}) custom-call(bf16[512,4096]{1,0:T(8,128)(2,1)S(1)} %get-tuple-element.24.x, bf16[4096,1024]{1,0:T(8,128)(2,1)S(1)} %get-tuple-element.25.wq, bf16[4,128,128]{2,1,0:T(8,128)(2,1)S(1)} %add_convert_fusion.1.after, bf16[1024,4096]{1,0:T(8,128)(2,1)} %w_hbm.3), custom_call_target="tpu_custom_call" | custom-call | flops 21474836 | bytes 83886 | tf_op jit(solution)/shard_map/queries/pallas_call | solution.py:208
  25.5 2.7 %collective-permute-start.4 = (bf16[4,128,128]{2,1,0:T(8,128)(2,1)S(1)}, bf16[4,128,128]{2,1,0:T(8,128)(2,1)S(1)}, u32[]{:S(2)}, u32[]{:S(2)}) collective-permute-start(bf16[4,128,128]{2,1,0:T(8,128)(2,1)S(1)} %add_convert_fusion.after), channel_id=1, source_target_pairs={{0,16},{4,20},{8,24},{12,28},{16,0},{20,4},{24,8},{28,12},{1,17},{... | collective-permute-start | bytes 393224 | tf_op jit(solution)/shard_map/ppermute | solution.py:356
  28.1 0.8 %collective-permute-start.2 = (bf16[4,128,128]{2,1,0:T(8,128)(2,1)S(1)}, bf16[4,128,128]{2,1,0:T(8,128)(2,1)S(1)}, u32[]{:S(2)}, u32[]{:S(2)}) collective-permute-start(bf16[4,128,128]{2,1,0:T(8,128)(2,1)S(1)} %get-tuple-element.34.after), channel_id=1, source_target_pairs={{0,4},{4,0},{8,12},{12,8},{16,20},{20,16},{24,28},{28,24},{1,5},{5... | collective-permute-start | bytes 393224 | tf_op jit(solution)/shard_map/ppermute | solution.py:356
  29.0 1.2 %collective-permute-start.3 = (bf16[4,128,128]{2,1,0:T(8,128)(2,1)S(1)}, bf16[4,128,128]{2,1,0:T(8,128)(2,1)S(1)}, u32[]{:S(2)}, u32[]{:S(2)}) collective-permute-start(bf16[4,128,128]{2,1,0:T(8,128)(2,1)S(1)} %collective-permute-done.1.refs_5_), channel_id=1, source_target_pairs={{0,4},{4,0},{8,12},{12,8},{16,20},{20,16},{24,28},{28,24},{1,5},{5... | collective-permute-start | bytes 393224 | tf_op jit(solution)/shard_map/ppermute | solution.py:356
  30.2 2.7 %attention.1.after.refs_2_ = f32[4,1024,128]{2,1,0:T(8,128)S(1)} custom-call(bf16[512,1024]{1,0:T(8,128)(2,1)S(1)} %get-tuple-element.22.k_ref, bf16[1024,512]{1,0:T(8,128)(2,1)S(1)} %get-tuple-element.23.vt_ref, f32[21,8,512]{2,1,0:T(8,128)S(1)} %get-tuple-element.27.lam_ref.refs_9_, f32[4,8,128,128]{3,2,1,0:T(8,128)S(1)} %get-tuple-element.28.prior_ref, ...), custom_call_target="tpu_custom_call" | custom-call | flops 8053063 | bytes 41943 | tf_op jit(solution)/shard_map/attention/pallas_call | solution.py:233
  32.9 1.9 %collective-permute-done.4.refs_7_ = bf16[4,128,128]{2,1,0:T(8,128)(2,1)S(1)} collective-permute-done((bf16[4,128,128]{2,1,0:T(8,128)(2,1)S(1)}, bf16[4,128,128]{2,1,0:T(8,128)(2,1)S(1)}, u32[]{:S(2)}, u32[]{:S(2)}) %collective-permute-start.4) | collective-permute-done | bytes 131104 | tf_op jit(solution)/shard_map/ppermute | solution.py:356
  34.8 0.8 %collective-permute-start.5 = (bf16[4,128,128]{2,1,0:T(8,128)(2,1)S(1)}, bf16[4,128,128]{2,1,0:T(8,128)(2,1)S(1)}, u32[]{:S(2)}, u32[]{:S(2)}) collective-permute-start(bf16[4,128,128]{2,1,0:T(8,128)(2,1)S(1)} %collective-permute-done.4.refs_7_), channel_id=1, source_target_pairs={{0,4},{4,0},{8,12},{12,8},{16,20},{20,16},{24,28},{28,24},{1,5},{5... | collective-permute-start | bytes 393224 | tf_op jit(solution)/shard_map/ppermute | solution.py:356
  35.7 0.6 collective-permute-done.3.refs_6_
  36.2 3.6 %collective-permute-done.5.refs_8_ = bf16[4,128,128]{2,1,0:T(8,128)(2,1)S(1)} collective-permute-done((bf16[4,128,128]{2,1,0:T(8,128)(2,1)S(1)}, bf16[4,128,128]{2,1,0:T(8,128)(2,1)S(1)}, u32[]{:S(2)}, u32[]{:S(2)}) %collective-permute-start.5) | collective-permute-done | bytes 131104 | tf_op jit(solution)/shard_map/ppermute | solution.py:356
  40.3 1.0 %far_part.3.after.refs_0_.refs_1_ = bf16[384,1024]{1,0:T(8,128)(2,1)S(1)} custom-call(bf16[128,1024]{1,0:T(8,128)(2,1)S(1)} %far_part.2.after.refs_0_, bf16[4,512,128]{2,1,0:T(8,128)(2,1)S(1)} %get-tuple-element.30.refs_0_, bf16[4,512,128]{2,1,0:T(8,128)(2,1)S(1)} %get-tuple-element.32.refs_1_, f32[4,1024,128]{2,1,0:T(8,128)S(1)} %attention.1.after.refs_2_, ...), custom_call_target="tpu_custom_call" | custom-call | flops 5368709 | bytes 41943 | tf_op jit(solution)/shard_map/far_part/pallas_call | solution.py:281
  41.3 0.6 collective-permute-start.8
  41.9 0.7 %project.3.after = bf16[128,1024]{1,0:T(8,128)(2,1)S(1)} custom-call(bf16[384,1024]{1,0:T(8,128)(2,1)S(1)} %far_part.3.after.refs_0_.refs_1_, bf16[2,1024,1024]{2,1,0:T(8,128)(2,1)S(1)} %get-tuple-element.36.w, bf16[2,1024,1024]{2,1,0:T(8,128)(2,1)S(1)} %collective-permute-done.6.w_twin, bf16[128,1024]{1,0:T(8,128)(2,1)S(1)} %far_part.2.after.refs_0_, ...), custom_call_target="tpu_custom_call" | custom-call | flops 40000000000 | bytes 100000000 | tf_op jit(solution)/shard_map/project/pallas_call | solution.py:309
  42.6 1.6 %collective-permute-start.9 = (bf16[128,1024]{1,0:T(8,128)(2,1)S(1)}, bf16[128,1024]{1,0:T(8,128)(2,1)S(1)}, u32[]{:S(2)}, u32[]{:S(2)}) collective-permute-start(bf16[128,1024]{1,0:T(8,128)(2,1)S(1)} %project.3.after), channel_id=1, source_target_pairs={{0,2},{1,3},{2,0},{3,1},{4,6},{5,7},{6,4},{7,5},{8,10},{9,11},{10,... | collective-permute-start | bytes 786440 | tf_op jit(solution)/shard_map/ppermute | solution.py:396
  44.2 1.8 %project.4.after = bf16[384,1024]{1,0:T(8,128)(2,1)S(1)} custom-call(bf16[128,1024]{1,0:T(8,128)(2,1)S(1)} %project.3.after, bf16[2,1024,1024]{2,1,0:T(8,128)(2,1)S(1)} %get-tuple-element.36.w, bf16[2,1024,1024]{2,1,0:T(8,128)(2,1)S(1)} %collective-permute-done.6.w_twin, bf16[384,1024]{1,0:T(8,128)(2,1)S(1)} %far_part.3.after.refs_0_.refs_1_, ...), custom_call_target="tpu_custom_call" | custom-call | flops 16106127 | bytes 41943 | tf_op jit(solution)/shard_map/project/pallas_call | solution.py:309
  46.0 1.2 %collective-permute-start.10 = (bf16[384,1024]{1,0:T(8,128)(2,1)S(1)}, bf16[384,1024]{1,0:T(8,128)(2,1)S(1)}, u32[]{:S(2)}, u32[]{:S(2)}) collective-permute-start(bf16[384,1024]{1,0:T(8,128)(2,1)S(1)} %project.4.after), channel_id=1, source_target_pairs={{0,2},{1,3},{2,0},{3,1},{4,6},{5,7},{6,4},{7,5},{8,10},{9,11},{10,... | collective-permute-start | bytes 2359304 | tf_op jit(solution)/shard_map/ppermute | solution.py:396
  47.2 2.3 %project.5.own_ref = f32[512,1024]{1,0:T(8,128)S(1)} custom-call(bf16[384,1024]{1,0:T(8,128)(2,1)S(1)} %project.4.after, bf16[2,1024,1024]{2,1,0:T(8,128)(2,1)S(1)} %get-tuple-element.36.w, bf16[2,1024,1024]{2,1,0:T(8,128)(2,1)S(1)} %collective-permute-done.6.w_twin, bf16[128,1024]{1,0:T(8,128)(2,1)S(1)} %far_part.2.after.refs_0_, ...), custom_call_target="tpu_custom_call" | custom-call | flops 21474836 | bytes 41943 | tf_op jit(solution)/shard_map/project/pallas_call | solution.py:309
  49.5 2.3 %collective-permute-done.9.refs_0_ = bf16[128,1024]{1,0:T(8,128)(2,1)S(1)} collective-permute-done((bf16[128,1024]{1,0:T(8,128)(2,1)S(1)}, bf16[128,1024]{1,0:T(8,128)(2,1)S(1)}, u32[]{:S(2)}, u32[]{:S(2)}) %collective-permute-start.9) | collective-permute-done | bytes 262176 | tf_op jit(solution)/shard_map/ppermute | solution.py:396
  51.8 0.7 %finish.2.out_in = bf16[512,1024]{1,0:T(8,128)(2,1)} custom-call(f32[1,1024]{1,0:T(1,128)S(1)} %bitcast.3, f32[512,1024]{1,0:T(8,128)S(1)} %project.5.own_ref, bf16[128,1024]{1,0:T(8,128)(2,1)S(1)} %collective-permute-done.9.refs_0_), custom_call_target="tpu_custom_call" | custom-call | flops 40000000000 | bytes 100000000 | tf_op jit(solution)/shard_map/finish/pallas_call | solution.py:331
  52.6 15.3 %collective-permute-done.10.refs_0_ = bf16[384,1024]{1,0:T(8,128)(2,1)S(1)} collective-permute-done((bf16[384,1024]{1,0:T(8,128)(2,1)S(1)}, bf16[384,1024]{1,0:T(8,128)(2,1)S(1)}, u32[]{:S(2)}, u32[]{:S(2)}) %collective-permute-start.10) | collective-permute-done | bytes 786464 | tf_op jit(solution)/shard_map/ppermute | solution.py:396
  67.9 1.5 %finish.3 = bf16[512,1024]{1,0:T(8,128)(2,1)} custom-call(bf16[512,1024]{1,0:T(8,128)(2,1)} %finish.2.out_in, f32[512,1024]{1,0:T(8,128)S(1)} %project.5.own_ref, bf16[384,1024]{1,0:T(8,128)(2,1)S(1)} %collective-permute-done.10.refs_0_), custom_call_target="tpu_custom_call", output_to_operand_aliasing={{}: (0, {})} | custom-call | flops 40000000000 | bytes 100000000 | tf_op jit(solution)/shard_map/finish/pallas_call | solution.py:331
  (13 shorter events, 0.8 us)
Async XLA Ops:
  12.0 7.4 %collective-permute-start = (bf16[4,128,128]{2,1,0:T(8,128)(2,1)S(1)}, bf16[4,128,128]{2,1,0:T(8,128)(2,1)S(1)}, u32[]{:S(2)}, u32[]{:S(2)}) collective-permute-start(bf16[4,128,128]{2,1,0:T(8,128)(2,1)S(1)} %get-tuple-element.29), channel_id=1, source_target_pairs={{0,4},{4,0},{8,12},{12,8},{16,20},{20,16},{24,28},{28,24},{1,5},{5... | collective-permute-start | bytes 393224 | tf_op jit(solution)/shard_map/ppermute | solution.py:356
  19.4 22.4 %collective-permute-start.6 = (bf16[2,1024,1024]{2,1,0:T(8,128)(2,1)S(1)}, bf16[2,1024,1024]{2,1,0:T(8,128)(2,1)S(1)}, u32[]{:S(2)}, u32[]{:S(2)}) collective-permute-start(bf16[2,1024,1024]{2,1,0:T(8,128)(2,1)S(1)} %get-tuple-element.38), channel_id=1, source_target_pairs={{0,1},{1,0},{2,3},{3,2},{4,5},{5,4},{6,7},{7,6},{8,9},{9,8},{10,11... | collective-permute-start | bytes 12582920 | tf_op jit(solution)/shard_map/ppermute | solution.py:375
  19.5 5.9 %collective-permute-start.1 = (bf16[4,128,128]{2,1,0:T(8,128)(2,1)S(1)}, bf16[4,128,128]{2,1,0:T(8,128)(2,1)S(1)}, u32[]{:S(2)}, u32[]{:S(2)}) collective-permute-start(bf16[4,128,128]{2,1,0:T(8,128)(2,1)S(1)} %add_convert_fusion.1.after), channel_id=1, source_target_pairs={{0,8},{4,12},{8,0},{12,4},{16,24},{20,28},{24,16},{28,20},{1,9},{5... | collective-permute-start | bytes 393224 | tf_op jit(solution)/shard_map/ppermute | solution.py:356
  25.4 14.4 %copy-start = (f32[1024]{0:T(1024)S(1)}, f32[1024]{0:T(1024)}, u32[]{:S(2)}) copy-start(f32[1024]{0:T(1024)} %param.13) | copy-start | bytes 12292
  25.5 9.3 %collective-permute-start.4 = (bf16[4,128,128]{2,1,0:T(8,128)(2,1)S(1)}, bf16[4,128,128]{2,1,0:T(8,128)(2,1)S(1)}, u32[]{:S(2)}, u32[]{:S(2)}) collective-permute-start(bf16[4,128,128]{2,1,0:T(8,128)(2,1)S(1)} %add_convert_fusion.after), channel_id=1, source_target_pairs={{0,16},{4,20},{8,24},{12,28},{16,0},{20,4},{24,8},{28,12},{1,17},{... | collective-permute-start | bytes 393224 | tf_op jit(solution)/shard_map/ppermute | solution.py:356
  28.1 7.5 %collective-permute-start.2 = (bf16[4,128,128]{2,1,0:T(8,128)(2,1)S(1)}, bf16[4,128,128]{2,1,0:T(8,128)(2,1)S(1)}, u32[]{:S(2)}, u32[]{:S(2)}) collective-permute-start(bf16[4,128,128]{2,1,0:T(8,128)(2,1)S(1)} %get-tuple-element.34.after), channel_id=1, source_target_pairs={{0,4},{4,0},{8,12},{12,8},{16,20},{20,16},{24,28},{28,24},{1,5},{5... | collective-permute-start | bytes 393224 | tf_op jit(solution)/shard_map/ppermute | solution.py:356
  29.0 7.2 %collective-permute-start.3 = (bf16[4,128,128]{2,1,0:T(8,128)(2,1)S(1)}, bf16[4,128,128]{2,1,0:T(8,128)(2,1)S(1)}, u32[]{:S(2)}, u32[]{:S(2)}) collective-permute-start(bf16[4,128,128]{2,1,0:T(8,128)(2,1)S(1)} %collective-permute-done.1.refs_5_), channel_id=1, source_target_pairs={{0,4},{4,0},{8,12},{12,8},{16,20},{20,16},{24,28},{28,24},{1,5},{5... | collective-permute-start | bytes 393224 | tf_op jit(solution)/shard_map/ppermute | solution.py:356
  34.8 5.0 %collective-permute-start.5 = (bf16[4,128,128]{2,1,0:T(8,128)(2,1)S(1)}, bf16[4,128,128]{2,1,0:T(8,128)(2,1)S(1)}, u32[]{:S(2)}, u32[]{:S(2)}) collective-permute-start(bf16[4,128,128]{2,1,0:T(8,128)(2,1)S(1)} %collective-permute-done.4.refs_7_), channel_id=1, source_target_pairs={{0,4},{4,0},{8,12},{12,8},{16,20},{20,16},{24,28},{28,24},{1,5},{5... | collective-permute-start | bytes 393224 | tf_op jit(solution)/shard_map/ppermute | solution.py:356
  40.3 1.6 %collective-permute-start.7 = (bf16[128,1024]{1,0:T(8,128)(2,1)S(1)}, bf16[128,1024]{1,0:T(8,128)(2,1)S(1)}, u32[]{:S(2)}, u32[]{:S(2)}) collective-permute-start(bf16[128,1024]{1,0:T(8,128)(2,1)S(1)} %far_part.2.after.refs_0_), channel_id=1, source_target_pairs={{0,1},{1,0},{2,3},{3,2},{4,5},{5,4},{6,7},{7,6},{8,9},{9,8},{10,11... | collective-permute-start | bytes 786440 | tf_op jit(solution)/shard_map/ppermute | solution.py:387
  41.3 2.9 %collective-permute-start.8 = (bf16[384,1024]{1,0:T(8,128)(2,1)S(1)}, bf16[384,1024]{1,0:T(8,128)(2,1)S(1)}, u32[]{:S(2)}, u32[]{:S(2)}) collective-permute-start(bf16[384,1024]{1,0:T(8,128)(2,1)S(1)} %far_part.3.after.refs_0_.refs_1_), channel_id=1, source_target_pairs={{0,1},{1,0},{2,3},{3,2},{4,5},{5,4},{6,7},{7,6},{8,9},{9,8},{10,11... | collective-permute-start | bytes 2359304 | tf_op jit(solution)/shard_map/ppermute | solution.py:389
  42.6 9.2 %collective-permute-start.9 = (bf16[128,1024]{1,0:T(8,128)(2,1)S(1)}, bf16[128,1024]{1,0:T(8,128)(2,1)S(1)}, u32[]{:S(2)}, u32[]{:S(2)}) collective-permute-start(bf16[128,1024]{1,0:T(8,128)(2,1)S(1)} %project.3.after), channel_id=1, source_target_pairs={{0,2},{1,3},{2,0},{3,1},{4,6},{5,7},{6,4},{7,5},{8,10},{9,11},{10,... | collective-permute-start | bytes 786440 | tf_op jit(solution)/shard_map/ppermute | solution.py:396
  46.0 21.9 %collective-permute-start.10 = (bf16[384,1024]{1,0:T(8,128)(2,1)S(1)}, bf16[384,1024]{1,0:T(8,128)(2,1)S(1)}, u32[]{:S(2)}, u32[]{:S(2)}) collective-permute-start(bf16[384,1024]{1,0:T(8,128)(2,1)S(1)} %project.4.after), channel_id=1, source_target_pairs={{0,2},{1,3},{2,0},{3,1},{4,6},{5,7},{6,4},{7,5},{8,10},{9,11},{10,... | collective-permute-start | bytes 2359304 | tf_op jit(solution)/shard_map/ppermute | solution.py:396
where the time goes:
time: 69.5 us; the launch traced here: 69.4 us
  Pallas kernels  31.8 us (46%)
  waiting for transfers between devices  23.7 us (34%)
  starting transfers between devices  13.6 us (20%)
    ppermute x2, waiting for transfers between devices, per_device(): lax.ppermute(after, 'head', [(i, (i + 2 * d) % groups) for i in range(gro...  17.6 us
    pallas_call x1, Pallas kernels, keys_values(): pl.pallas_call(functools.partial(keys_values_body, width), in_specs=[HBM]...  12 us
    ppermute x6, starting transfers between devices, send(): return lax.ppermute(state, 'seq', [(r, r ^ 1 << j) for r in range(count)])  10.2 us
    pallas_call x2, Pallas kernels, queries(): pl.pallas_call(functools.partial(queries_body, width, part, flip, len(fet...  8.59 us
    ppermute x6, waiting for transfers between devices, send(): return lax.ppermute(state, 'seq', [(r, r ^ 1 << j) for r in range(count)])  6.04 us
    pallas_call x3, Pallas kernels, project(): pl.pallas_call(functools.partial(project_body, d, len(mine)), in_specs=[A...  4.84 us
    pallas_call x1, Pallas kernels, attention(): pl.pallas_call(functools.partial(attention_body, width, len(queries_t)),...  2.74 us
    ppermute x2, starting transfers between devices, per_device(): lax.ppermute(after, 'head', [(i, (i + 2 * d) % groups) for i in range(gro...  2.74 us
  transfers between devices with their start and end apart: 11, of which 5 were waited for; matrix products, arithmetic and copies ran while one was open for 0% of the time, Pallas kernels for 26%

commit v1 on v0

--- a/solution.py
+++ b/solution.py
@@ -52,7 +52,8 @@
     x_in = [pltpu.make_async_copy(x_hbm.at[:, a], x.at[:, a], sem.at[0, c]) for c, a in enumerate(at)]
     v_in = [pltpu.make_async_copy(wv_hbm.at[a], wv.at[a], sem.at[1, c]) for c, a in enumerate(at)]
     k_in = [pltpu.make_async_copy(wk_hbm.at[a], wk.at[a], sem.at[2, c]) for c, a in enumerate(at)]
-    q_in = [pltpu.make_async_copy(wq_hbm.at[a], wq.at[a], sem.at[3, c]) for c, a in enumerate(at)]
+    first_half = pl.ds(0, size // 2)
+    q_in = [pltpu.make_async_copy(wq_hbm.at[a, first_half], wq.at[a], sem.at[3, c]) for c, a in enumerate(at)]
     for c in range(cuts):
         starts((x_in[c], v_in[c]))
     starts(k_in)
@@ -96,7 +97,7 @@
         out_specs=[VMEM] * 6,
         out_shape=[
             pltpu.VMEM((rows, depth), bf16),
-            pltpu.VMEM((depth, size), bf16),
+            pltpu.VMEM((depth, size // 2), bf16),
             pltpu.VMEM((rows, size), bf16),
             pltpu.VMEM((size, rows), bf16),
             part,
@@ -165,97 +166,169 @@
     return pieces
 
 
-def attend_into(acc_ref, at, head, h, width, qt, k_ref, vt_ref, lam_ref, prior_ref):
-    own = slice(h * width, (h + 1) * width)
-    prior = [prior_ref[p, h] for p in range(prior_ref.shape[0])]
-    pieces = attend(qt, k_ref[:, own], vt_ref[own, :], lam_ref[:, head, :], prior)
-    for i, piece in enumerate(pieces):
-        acc_ref[i, at * width : (at + 1) * width, :] = piece
-
-
 def whole(qt_ref, at):
     return jnp.concatenate([qt_ref[i, at, :] for i in range(qt_ref.shape[0])], axis=1)
 
 
-def queries_body(width, part, flip, count, x, wq, after, w_hbm, *refs):
-    sources, qt_ref, w_ref, targets, sem = refs[:count], refs[count], refs[count + 1], refs[count + 2 : -1], refs[-1]
-    copies = [pltpu.make_async_copy(a, b, sem.at[n]) for n, (a, b) in enumerate(zip(sources, targets))]
-    chips, _, columns = w_ref.shape
-    group = lax.axis_index("head") ^ flip
-    for d in range(chips):
-        base = pl.multiple_of(lax.rem(group + 2 * d, 2 * chips) * columns, 128)
-        copies.append(pltpu.make_async_copy(w_hbm.at[:, pl.ds(base, columns)], w_ref.at[d], sem.at[count + d]))
+def finished(raw):
+    raw = raw.T
+    return (raw * lax.rsqrt(jnp.sum(raw * raw, axis=0, keepdims=True) + eps)).astype(bf16)
+
+
+def leave_tiles(ref, at, qt):
+    for i in range(ref.shape[0]):
+        ref[i, at, :] = qt[:, i * TILE : (i + 1) * TILE]
+
+
+def row_copies(source, first, target, sem, at, pieces):
+    cut = target.shape[0] // pieces
+    return [
+        pltpu.make_async_copy(source.at[pl.ds(first + c * cut, cut)], target.at[pl.ds(c * cut, cut)], sem.at[at + c])
+        for c in range(pieces)
+    ]
+
+
+def query_product(x, wq, raw_ref, meanwhile):
+    rows, depth = x.shape
+    cuts = 8
+    cut = depth // cuts
+    for c in range(cuts):
+        a = slice(c * cut, (c + 1) * cut)
+        term = mm(x[:, a], wq[a, :])
+        raw_ref[...] = term if c == 0 else raw_ref[...] + term
+        meanwhile(c, cuts)
+
+
+def queries_first_body(x, wq, wq_hbm, lam_hbm, prior_hbm, after, raw_ref, wq_next, lam, prior, sem):
+    depth, size = wq.shape
+    cut = depth // 8
+    copies = [pltpu.make_async_copy(lam_hbm, lam, sem.at[0])]
+    for c in range(8):
+        a = pl.ds(c * cut, cut)
+        copies.append(pltpu.make_async_copy(wq_hbm.at[a, pl.ds(size, size)], wq_next.at[a], sem.at[1 + c]))
+    for p in range(prior.shape[0]):
+        copies.append(pltpu.make_async_copy(prior_hbm.at[p], prior.at[p], sem.at[9 + p]))
     starts(copies)
-    rows = x.shape[0]
-    size = qt_ref.shape[1]
-    step = min(256, size)
-    for first in range(0, size, step):
-        raw_step = mm(x[...], wq[:, part * size + first : part * size + first + step])
-        for h in range(step // width):
-            raw = raw_step[:, h * width : (h + 1) * width].T
-            qt = (raw * lax.rsqrt(jnp.sum(raw * raw, axis=0, keepdims=True) + eps)).astype(bf16)
-            own = slice(first + h * width, first + (h + 1) * width)
-            for i in range(rows // TILE):
-                qt_ref[i, own, :] = qt[:, i * TILE : (i + 1) * TILE]
+    query_product(x, wq, raw_ref, lambda c, cuts: None)
     for copy in copies:
         copy.wait()
 
 
-def queries(tokens, w_query, after, w_out, flip, chips, width, part, fetch=()):
+def queries_first(tokens, half_query, w_query, level_weights, prior_states, after):
     rows, depth = tokens.shape
-    size = w_query.shape[1] // 2
-    columns = w_out.shape[1] // (2 * chips)
-    return pl.pallas_call(
-        functools.partial(queries_body, width, part, flip, len(fetch)),
-        in_specs=[VMEM, VMEM, ANY, HBM] + [HBM] * len(fetch),
-        out_specs=[VMEM] * (2 + len(fetch)),
-        out_shape=[pltpu.VMEM((rows // TILE, size, TILE), bf16), pltpu.VMEM((chips, w_out.shape[0], columns), bf16)]
-        + [pltpu.VMEM(a.shape, a.dtype) for a in fetch],
-        scratch_shapes=[pltpu.SemaphoreType.DMA((len(fetch) + chips,))],
+    size = half_query.shape[1]
+    return pl.pallas_call(
+        queries_first_body,
+        in_specs=[VMEM, VMEM, HBM, HBM, HBM, ANY],
+        out_specs=[VMEM] * 4,
+        out_shape=[
+            pltpu.VMEM((rows, size), f32),
+            pltpu.VMEM(half_query.shape, bf16),
+            pltpu.VMEM(level_weights.shape, f32),
+            pltpu.VMEM(prior_states.shape, f32),
+        ],
+        scratch_shapes=[pltpu.SemaphoreType.DMA((9 + prior_states.shape[0],))],
         compiler_params=params(16),
         cost_estimate=cost(2 * rows * depth * size, 2 * (rows * depth + depth * size)),
-        name="queries",
-    )(tokens, w_query, after, in_hbm(w_out), *[in_hbm(a) for a in fetch])
-
-
-def attention_body(width, halves, k_ref, vt_ref, lam_ref, prior_ref, after, *refs):
-    qt_refs, acc_ref = refs[:halves], refs[halves]
+        name="queries_first",
+    )(tokens, half_query, in_hbm(w_query), in_hbm(level_weights), in_hbm(prior_states), after)
+
+
+def queries_second_body(width, x, wq, raw_old, w_hbm, after, qt_ref, raw_ref, w_ref, sem):
+    copies = row_copies(w_hbm, 0, w_ref, sem, 0, 8)
+    starts(copies)
+    heads = raw_old.shape[1] // width
+
+    def meanwhile(c, cuts):
+        for h in range(c * heads // cuts, (c + 1) * heads // cuts):
+            own = slice(h * width, (h + 1) * width)
+            leave_tiles(qt_ref, own, finished(raw_old[:, own]))
+
+    query_product(x, wq, raw_ref, meanwhile)
+    for copy in copies:
+        copy.wait()
+
+
+def queries_second(tokens, half_query, raw_old, w_out, after, width):
+    rows, depth = tokens.shape
+    size = half_query.shape[1]
+    return pl.pallas_call(
+        functools.partial(queries_second_body, width),
+        in_specs=[VMEM, VMEM, VMEM, HBM, ANY],
+        out_specs=[VMEM] * 3,
+        out_shape=[
+            pltpu.VMEM((rows // TILE, size, TILE), bf16),
+            pltpu.VMEM((rows, size), f32),
+            pltpu.VMEM((w_out.shape[0] // 2, w_out.shape[1]), bf16),
+        ],
+        scratch_shapes=[pltpu.SemaphoreType.DMA((8,))],
+        compiler_params=params(16),
+        cost_estimate=cost(2 * rows * depth * size, 2 * (rows * depth + depth * size)),
+        name="queries_second",
+    )(tokens, half_query, raw_old, in_hbm(w_out), after)
+
+
+def attention_body(width, lam_ref, prior_ref, w_hbm, after, qt_old, raw, k_ref, vt_ref, acc_ref, qt_ref, w_ref, sem):
+    copies = row_copies(w_hbm, w_ref.shape[0], w_ref, sem, 0, 8)
+    starts(copies)
     heads = prior_ref.shape[1]
-    per = heads // halves
+    per = heads // 2
     for h in range(heads):
-        qt = whole(qt_refs[h // per], slice(h % per * width, (h % per + 1) * width))
-        attend_into(acc_ref, h, h, h, width, qt, k_ref, vt_ref, lam_ref, prior_ref)
-
-
-def attention(queries_t, keys, values_t, level_weights, prior_states, after, width):
-    tiles, _, take = queries_t[0].shape
-    total = keys.shape[1]
-    return pl.pallas_call(
-        functools.partial(attention_body, width, len(queries_t)),
-        in_specs=[VMEM] * 4 + [ANY] + [VMEM] * len(queries_t),
-        out_specs=VMEM,
-        out_shape=pltpu.VMEM((tiles, total, take), f32),
+        own = slice(h % per * width, (h % per + 1) * width)
+        every = slice(h * width, (h + 1) * width)
+        if h < per:
+            qt = whole(qt_old, own)
+        else:
+            qt = finished(raw[:, own])
+            leave_tiles(qt_ref, own, qt)
+        prior = [prior_ref[p, h] for p in range(prior_ref.shape[0])]
+        pieces = attend(qt, k_ref[:, every], vt_ref[every, :], lam_ref[:, h, :], prior)
+        for i, piece in enumerate(pieces):
+            acc_ref[i, every, :] = piece
+    for copy in copies:
+        copy.wait()
+
+
+def attention(qt_old, raw, keys, values_t, level_weights, prior_states, w_out, after, width):
+    tiles, size, take = qt_old.shape
+    return pl.pallas_call(
+        functools.partial(attention_body, width),
+        in_specs=[VMEM] * 2 + [HBM, ANY] + [VMEM] * 4,
+        out_specs=[VMEM] * 3,
+        out_shape=[
+            pltpu.VMEM((tiles, 2 * size, take), f32),
+            pltpu.VMEM(qt_old.shape, bf16),
+            pltpu.VMEM((w_out.shape[0] // 2, w_out.shape[1]), bf16),
+        ],
+        scratch_shapes=[pltpu.SemaphoreType.DMA((8,))],
         compiler_params=params(16),
-        cost_estimate=cost(12 * tiles * take * width * total, 8 * tiles * take * total),
+        cost_estimate=FAR_APART,
         name="attention",
-    )(keys, values_t, level_weights, prior_states, after, *queries_t)
-
-
-def far_body(width, first_level, halves, nbits, first, number, after, *refs):
-    qt_refs = refs[:halves]
-    acc_ref = refs[halves]
-    state_refs = refs[halves + 1 : halves + 1 + 2 * nbits]
-    lam_ref, gain_ref, out_ref = refs[halves + 1 + 2 * nbits :]
+    )(level_weights, prior_states, in_hbm(w_out), after, qt_old, raw, keys, values_t)
+
+
+def far_body(width, first_level, halves, counts, first, number, after, *refs):
+    refs = list(refs)
+    qt_refs = [refs.pop(0) for _ in range(halves)]
+    acc_ref = refs.pop(0)
+    arrived = [[refs.pop(0) for _ in range(count)] for count in counts]
+    lam_ref, gain_ref, out_ref = refs
+    nbits = len(counts) // 2
     heads = lam_ref.shape[1]
     half = heads // 2
     per = heads // halves
     mine = lax.axis_index("seq")
     odd = (mine & 1) > 0
+
+    def state(pieces, n):
+        each = pieces[0].shape[0]
+        return pieces[n // each][n % each]
+
     for head in range(heads):
         own = slice(head * width, (head + 1) * width)
         states = []
         for j in range(nbits):
-            kept, swapped = state_refs[2 * j][head % half], state_refs[2 * j + 1][head % half]
+            kept, swapped = state(arrived[2 * j], head % half), state(arrived[2 * j + 1], head % half)
             if j == 0:
                 states.append(kept if head >= half else swapped)
             else:
@@ -278,8 +351,10 @@
     levels, heads, rows = level_weights.shape
     total = heads * width
     halves = len(queries_t)
-    return pl.pallas_call(
-        functools.partial(far_body, width, rows.bit_length(), halves, len(states) // 2, first, number),
+    counts = [len(pieces) for pieces in states]
+    states = [piece for pieces in states for piece in pieces]
+    return pl.pallas_call(
+        functools.partial(far_body, width, rows.bit_length(), halves, counts, first, number),
         in_specs=[ANY] + [VMEM] * (halves + 3 + len(states)),
         out_specs=VMEM,
         out_shape=pltpu.VMEM((number * TILE, total), bf16),
@@ -289,49 +364,56 @@
     )(after, *queries_t, acc, *states, level_weights, gain)
 
 
-def project_body(d, count, after, w, w_twin, *refs):
-    mine, twins, out_ref = refs[:count], refs[count : 2 * count], refs[2 * count]
-    columns = w.shape[2]
-    step = min(256, columns)
+def project_body(flip, d, groups, start, take, count, after, w_top, w_low, *refs):
+    pieces, added, out_ref = refs[:count], refs[count:-1], refs[-1]
+    columns = out_ref.shape[1]
+    depth = w_top.shape[0]
+    base = lax.rem((lax.axis_index("head") ^ flip) + 2 * d, groups) * columns
+    step = min(512, columns)
     for first in range(0, columns, step):
         here = slice(first, first + step)
+        there = pl.ds(pl.multiple_of(base + first, 128), step)
+        top, low = w_top[:, there], w_low[:, there]
         row = 0
-        for a, b in zip(mine, twins):
-            take = a.shape[0]
-            total = mm(a[...], w[d, :, here]) + mm(b[...], w_twin[d, :, here])
-            out_ref[row : row + take, here] = total.astype(out_ref.dtype)
-            row += take
-
-
-def project(after, w, w_twin, mine, twins, kind, d, estimate=None):
-    _, depth, columns = w.shape
-    take = sum(a.shape[0] for a in mine)
-    return pl.pallas_call(
-        functools.partial(project_body, d, len(mine)),
-        in_specs=[ANY, VMEM, VMEM] + [VMEM] * (2 * len(mine)),
+        for a in pieces:
+            some = take or a.shape[0]
+            total = mm(a[start : start + some, :depth], top) + mm(a[start : start + some, depth:], low)
+            for ref in added:
+                total = total + ref[start : start + some, here].astype(f32)
+            out_ref[row : row + some, here] = total.astype(out_ref.dtype)
+            row += some
+
+
+def project(after, weights, flip, d, groups, pieces, kind, start=0, take=None, added=(), estimate=None):
+    depth, columns = weights[0].shape
+    columns //= groups
+    total = take or sum(a.shape[0] for a in pieces)
+    return pl.pallas_call(
+        functools.partial(project_body, flip, d, groups, start, take, len(pieces)),
+        in_specs=[ANY, VMEM, VMEM] + [VMEM] * (len(pieces) + len(added)),
         out_specs=VMEM,
-        out_shape=pltpu.VMEM((take, columns), kind),
+        out_shape=pltpu.VMEM((total, columns), kind),
         compiler_params=params(16),
-        cost_estimate=estimate or cost(4 * take * depth * columns, 4 * depth * columns),
+        cost_estimate=estimate or cost(4 * total * depth * columns, 4 * depth * columns),
         name="project",
-    )(after, w, w_twin, *mine, *twins)
-
-
-def finish_body(count, out_in, own_ref, *refs):
+    )(after, *weights, *pieces, *added)
+
+
+def finish_body(out_in, own_ref, *refs):
     out_ref = refs[-1]
     total = own_ref[...]
-    for ref in refs[:count]:
+    for ref in refs[:-1]:
         total = total + ref[...].astype(f32)
     out_ref[...] = total.astype(bf16)
 
 
-def finish(out, own, terms, first):
+def finish(out, own, other, terms, first):
     rows, columns = own.shape
     place = lambda i: (first // TILE + i, 0)
     return pl.pallas_call(
-        functools.partial(finish_body, len(terms)),
+        finish_body,
         grid=(terms[0].shape[0] // TILE,),
-        in_specs=[ANY, pl.BlockSpec((TILE, columns), place)]
+        in_specs=[ANY] + [pl.BlockSpec((TILE, columns), place)] * 2
         + [pl.BlockSpec((TILE, columns), lambda i: (i, 0))] * len(terms),
         out_specs=pl.BlockSpec((TILE, columns), place),
         out_shape=jax.ShapeDtypeStruct((rows, columns), bf16),
@@ -339,7 +421,7 @@
         compiler_params=params(16),
         cost_estimate=FAR_APART,
         name="finish",
-    )(out, own, *terms)
+    )(out, own, other, *terms)
 
 
 def per_device(tokens, w_query, w_key, w_value, w_out, norm_gain, level_weights, prior_states):
@@ -361,43 +443,64 @@
     def not_before(value, done):
         return lax.optimization_barrier((value, done))[0]
 
-    tokens, w_query, keys, values_t, keep, give = keys_values(tokens, w_key, w_value, w_query, width)
+    tokens, half_query, keys, values_t, keep, give = keys_values(tokens, w_key, w_value, w_query, width)
     got = send(give, 0)
-    q_a, w_give, level_weights, prior_states = queries(
-        tokens, w_query, keep, w_out, 1, chips, width, 0, (level_weights, prior_states)
+    raw_a, next_query, level_weights, prior_states = queries_first(
+        tokens, half_query, w_query, level_weights, prior_states, keep
     )
-    got = not_before(got, q_a)
+    got = not_before(got, raw_a)
     running = merge(keep, got)
-    states = [got]
+    kept, swapped = [[got]], []
     for j in range(1, nbits):
-        got = send(running, j)
+        cut = running.shape[0]
+        gots = [send(running[n : n + cut], j) for n in range(0, running.shape[0], cut)]
         if j == 1:
-            w_twin = lax.ppermute(not_before(w_give, running), "head", twin)
-            states.append(send(not_before(keep, running), 0))
-            done, w = queries(tokens, w_query, running, w_out, 0, chips, width, 1)
-            queries_t = [q_a, done]
-        elif j == nbits - 1:
-            done = acc = attention(queries_t, keys, values_t, level_weights, prior_states, running, width)
-        got = not_before(got, done)
+            q_a, done, w_top = queries_second(tokens, next_query, raw_a, w_out, running, width)
+        if j == nbits - 1:
+            acc, q_b, w_low = attention(
+                q_a, done, keys, values_t, level_weights, prior_states, w_out, running, width
+            )
+            swapped = [[send(not_before(keep, running), 0)]] + [[send(not_before(old[0], running), 0)] for old in kept[1:]]
+            done = acc
+        gots = [not_before(got, done) for got in gots]
         if j < nbits - 1:
-            running = merge(running, got)
-        states += [got, send(got, 0)]
-
-    first = far_part(acc, queries_t, acc, states, level_weights, gain, width, 0, 1)
-    first_twin = lax.ppermute(first, "head", twin)
-    rest = far_part(first, queries_t, acc, states, level_weights, gain, width, 1, rows // TILE - 1)
-    rest_twin = lax.ppermute(rest, "head", twin)
-    after = rest
+            running = merge(running, gots[0])
+        kept.append(gots)
+    swapped.append([send(got, 0) for got in kept[-1]])
+    states = [pieces for pair in zip(kept, swapped) for pieces in pair]
+    queries_t = [q_a, q_b]
+    weights = (w_top, w_low)
+
+    def shared(after, piece):
+        gots = []
+        for d in range(1, chips):
+            after = project(after, weights, 1, d, groups, [piece], bf16)
+            gots.append(lax.ppermute(after, "head", twin))
+        return after, gots
+
     received = []
-    for mine, other, estimate in ((first, first_twin, FAR_APART), (rest, rest_twin, None)):
+
+    def onward(after, piece, gots, start, take, estimate=None):
         terms = []
         for d in range(1, chips):
-            after = project(after, w, w_twin, [mine], [other], bf16, d, estimate)
+            after = project(after, weights, 0, d, groups, [piece], bf16, start, take, gots[d - 1 : d], estimate)
             terms.append(lax.ppermute(after, "head", [(i, (i + 2 * d) % groups) for i in range(groups)]))
         received.append(terms)
-    own = project(after, w, w_twin, [first, rest], [first_twin, rest_twin], f32, 0)
-    out = finish(gain, own, received[0], 0)
-    return finish(out, own, received[1], TILE)
+        return after
+
+    ahead = far_part(acc, queries_t, acc, states, level_weights, gain, width, 0, 1)
+    after, ahead_gots = shared(ahead, ahead)
+    rest = far_part(after, queries_t, acc, states, level_weights, gain, width, 1, rows // TILE - 1)
+    after = onward(rest, ahead, ahead_gots, 0, TILE)
+    after, rest_gots = shared(after, rest)
+    after = project(after, weights, 1, 0, groups, [ahead, rest], bf16, estimate=FAR_APART)
+    other = lax.ppermute(after, "head", twin)
+    after = onward(after, rest, rest_gots, 0, rows - 2 * TILE, FAR_APART)
+    after = onward(after, rest, rest_gots, rows - 2 * TILE, TILE)
+    own = project(after, weights, 0, 0, groups, [ahead, rest], f32)
+    out = finish(gain, own, other, received[0], 0)
+    out = finish(out, own, other, received[1], TILE)
+    return finish(out, own, other, received[2], rows - TILE)
 
 
 def solution(mesh):

time: 69.5 us -> 69.3 us (level)
  waiting for transfers between devices: 23.7 us -> 19.5 us
  Pallas kernels: 31.8 us -> 35.1 us
  starting transfers between devices: 13.6 us -> 14.3 us
    pallas_call x8 -> x13, Pallas kernels: 18.4 us -> 21.5 us  [the longest x7 5.62 us: project(): pl.pallas_call(functools.partial(project_body, flip, d, groups, start, ta...]
    ppermute x5 -> x6, waiting for transfers between devices: 17.6 us -> 15.1 us  [the longest x3 14.1 us: onward(): lax.ppermute(after, 'head', [(i, (i + 2 * d) % groups) for i in range(gro...]
    ppermute x6, waiting for transfers between devices: 6.04 us -> 4.48 us  [send(): return lax.ppermute(state, 'seq', [(r, r ^ 1 << j) for r in range(count)])]
    ppermute x5 -> x6, starting transfers between devices: 3.44 us -> 4.4 us  [the longest x3 3.71 us: onward(): lax.ppermute(after, 'head', [(i, (i + 2 * d) % groups) for i in range(gro...]
  transfers between devices with their start and end apart: 11 -> 12, of which waited for: 5 -> 6; matrix products, arithmetic and copies ran while one was open for 0% -> 0% of each run, Pallas kernels for 26% -> 30%
where the time goes in v1:
time: 69.3 us; the launch traced here: 69.2 us
  Pallas kernels  35.1 us (51%)
  waiting for transfers between devices  19.5 us (28%)
  starting transfers between devices  14.3 us (21%)
    ppermute x3, waiting for transfers between devices, onward(): lax.ppermute(after, 'head', [(i, (i + 2 * d) % groups) for i in range(gro...  14.1 us
    pallas_call x1, Pallas kernels, keys_values(): pl.pallas_call(functools.partial(keys_values_body, width), in_specs=[HBM]...  12 us
    ppermute x6, starting transfers between devices, send(): return lax.ppermute(state, 'seq', [(r, r ^ 1 << j) for r in range(count)])  9.92 us
    pallas_call x7, Pallas kernels, project(): pl.pallas_call(functools.partial(project_body, flip, d, groups, start, ta...  5.62 us
    pallas_call x1, Pallas kernels, queries_first(): pl.pallas_call(queries_first_body, in_specs=[VMEM, VMEM, HBM, HBM, HBM, A...  4.74 us
    ppermute x6, waiting for transfers between devices, send(): return lax.ppermute(state, 'seq', [(r, r ^ 1 << j) for r in range(count)])  4.48 us
    pallas_call x1, Pallas kernels, attention(): pl.pallas_call(functools.partial(attention_body, width), in_specs=[VMEM]...  4.46 us
    pallas_call x1, Pallas kernels, queries_second(): pl.pallas_call(functools.partial(queries_second_body, width), in_specs=[V...  4.21 us
  transfers between devices with their start and end apart: 12, of which 6 were waited for; matrix products, arithmetic and copies ran while one was open for 0% of the time, Pallas kernels for 30%

profile of v1, /device:TPU:0, one launch (start us, length us, event | category | flops | bytes accessed | tf_op | source)
XLA Modules:
  0.0 69.2 jit_solution(12914598745984208713)
XLA Ops:
  0.0 12.0 %keys_values.1 = (bf16[512,4096]{1,0:T(8,128)(2,1)S(1)}, bf16[4096,512]{1,0:T(8,128)(2,1)S(1)}, bf16[512,1024]{1,0:T(8,128)(2,1)S(1)}, bf16[1024,512]{1,0:T(8,12...) custom-call(bf16[512,4096]{1,0:T(8,128)(2,1)} %x_hbm.1, bf16[4096,1024]{1,0:T(8,128)(2,1)} %wk_hbm.1, ...), custom_call_target="tpu_custom_call" | custom-call | flops 85899344 | bytes 209715 | tf_op jit(solution)/shard_map/keys_values/pallas_call | solution.py:94
  12.0 3.0 %collective-permute-start = (bf16[4,128,128]{2,1,0:T(8,128)(2,1)S(1)}, bf16[4,128,128]{2,1,0:T(8,128)(2,1)S(1)}, u32[]{:S(2)}, u32[]{:S(2)}) collective-permute-start(bf16[4,128,128]{2,1,0:T(8,128)(2,1)S(1)} %get-tuple-element.31), channel_id=1, source_target_pairs={{0,4},{4,0},{8,12},{12,8},{16,20},{20,16},{24,28},{28,24},{1,5},{5... | collective-permute-start | bytes 393224 | tf_op jit(solution)/shard_map/ppermute | solution.py:438
  15.0 4.7 %queries_first.1 = (f32[512,512]{1,0:T(8,128)S(1)}, bf16[4096,512]{1,0:T(8,128)(2,1)S(1)}, f32[21,8,512]{2,1,0:T(8,128)S(1)}, f32[4,8,128,128]{3,2,1,0:T(8,128)S(1)}) custom-call(bf16[512,4096]{1,0:T(8,128)(2,1)S(1)} %get-tuple-element.26.x, bf16[4096,512]{1,0:T(8,128)(2,1)S(1)} %get-tuple-element.27.wq, bf16[4096,1024]{1,0:T(8,128)(2,1)} %wq_hbm.3, ...), custom_call_target="tpu_custom_call" | custom-call | flops 21474836 | bytes 83886 | tf_op jit(solution)/shard_map/queries_first/pallas_call | solution.py:220
  19.8 1.6 %collective-permute-start.1 = (bf16[4,128,128]{2,1,0:T(8,128)(2,1)S(1)}, bf16[4,128,128]{2,1,0:T(8,128)(2,1)S(1)}, u32[]{:S(2)}, u32[]{:S(2)}) collective-permute-start(bf16[4,128,128]{2,1,0:T(8,128)(2,1)S(1)} %add_convert_fusion.1.after), channel_id=1, source_target_pairs={{0,8},{4,12},{8,0},{12,4},{16,24},{20,28},{24,16},{28,20},{1,9},{5... | collective-permute-start | bytes 393224 | tf_op jit(solution)/shard_map/ppermute | solution.py:438
  21.5 4.2 %queries_second.1 = (bf16[4,512,128]{2,1,0:T(8,128)(2,1)S(1)}, f32[512,512]{1,0:T(8,128)S(1)}, bf16[512,4096]{1,0:T(8,128)(2,1)S(1)}) custom-call(bf16[512,4096]{1,0:T(8,128)(2,1)S(1)} %get-tuple-element.26.x, bf16[4096,512]{1,0:T(8,128)(2,1)S(1)} %get-tuple-element.34.wq, f32[512,512]{1,0:T(8,128)S(1)} %get-tuple-element.32.raw_old, ...), custom_call_target="tpu_custom_call" | custom-call | flops 21474836 | bytes 83886 | tf_op jit(solution)/shard_map/queries_second/pallas_call | solution.py:255
  25.7 2.7 %collective-permute-start.4 = (bf16[4,128,128]{2,1,0:T(8,128)(2,1)S(1)}, bf16[4,128,128]{2,1,0:T(8,128)(2,1)S(1)}, u32[]{:S(2)}, u32[]{:S(2)}) collective-permute-start(bf16[4,128,128]{2,1,0:T(8,128)(2,1)S(1)} %add_convert_fusion.after), channel_id=1, source_target_pairs={{0,16},{4,20},{8,24},{12,28},{16,0},{20,4},{24,8},{28,12},{1,17},{... | collective-permute-start | bytes 393224 | tf_op jit(solution)/shard_map/ppermute | solution.py:438
  28.9 1.5 %collective-permute-start.3 = (bf16[4,128,128]{2,1,0:T(8,128)(2,1)S(1)}, bf16[4,128,128]{2,1,0:T(8,128)(2,1)S(1)}, u32[]{:S(2)}, u32[]{:S(2)}) collective-permute-start(bf16[4,128,128]{2,1,0:T(8,128)(2,1)S(1)} %collective-permute-done.1.refs_5_), channel_id=1, source_target_pairs={{0,4},{4,0},{8,12},{12,8},{16,20},{20,16},{24,28},{28,24},{1,5},{5... | collective-permute-start | bytes 393224 | tf_op jit(solution)/shard_map/ppermute | solution.py:438
  30.4 4.5 %attention.1 = (f32[4,1024,128]{2,1,0:T(8,128)S(1)}, bf16[4,512,128]{2,1,0:T(8,128)(2,1)S(1)}, bf16[512,4096]{1,0:T(8,128)(2,1)S(1)}) custom-call(f32[21,8,512]{2,1,0:T(8,128)S(1)} %get-tuple-element.29.lam_ref.refs_9_, f32[4,8,128,128]{3,2,1,0:T(8,128)S(1)} %get-tuple-element.30.prior_ref, bf16[1024,4096]{1,0:T(8,128)(2,1)} %w_hbm.3, ...), custom_call_target="tpu_custom_call" | custom-call | flops 40000000000 | bytes 100000000 | tf_op jit(solution)/shard_map/attention/pallas_call | solution.py:294
  34.9 0.6 collective-permute-start.5
  35.6 4.3 %collective-permute-done.5.refs_8_ = bf16[4,128,128]{2,1,0:T(8,128)(2,1)S(1)} collective-permute-done((bf16[4,128,128]{2,1,0:T(8,128)(2,1)S(1)}, bf16[4,128,128]{2,1,0:T(8,128)(2,1)S(1)}, u32[]{:S(2)}, u32[]{:S(2)}) %collective-permute-start.5) | collective-permute-done | bytes 131104 | tf_op jit(solution)/shard_map/ppermute | solution.py:438
  39.9 0.7 far_part.2.after.refs_0_
  41.2 1.0 %far_part.3.after.refs_0_.refs_1_ = bf16[384,1024]{1,0:T(8,128)(2,1)S(1)} custom-call(bf16[128,1024]{1,0:T(8,128)(2,1)S(1)} %project.7.after, bf16[4,512,128]{2,1,0:T(8,128)(2,1)S(1)} %get-tuple-element.37.qt_old.refs_0_, bf16[4,512,128]{2,1,0:T(8,128)(2,1)S(1)} %get-tuple-element.41.refs_1_, f32[4,1024,128]{2,1,0:T(8,128)S(1)} %get-tuple-element.40.after.refs_2_, ...), custom_call_target="tpu_custom_call" | custom-call | flops 5368709 | bytes 41943 | tf_op jit(solution)/shard_map/far_part/pallas_call | solution.py:356
  43.1 1.6 %collective-permute-start.9 = (bf16[128,1024]{1,0:T(8,128)(2,1)S(1)}, bf16[128,1024]{1,0:T(8,128)(2,1)S(1)}, u32[]{:S(2)}, u32[]{:S(2)}) collective-permute-start(bf16[128,1024]{1,0:T(8,128)(2,1)S(1)} %project.8.after), channel_id=1, source_target_pairs={{0,2},{1,3},{2,0},{3,1},{4,6},{5,7},{6,4},{7,5},{8,10},{9,11},{10,... | collective-permute-start | bytes 786440 | tf_op jit(solution)/shard_map/ppermute | solution.py:487
  44.7 1.0 %project.9.after = bf16[384,1024]{1,0:T(8,128)(2,1)S(1)} custom-call(bf16[128,1024]{1,0:T(8,128)(2,1)S(1)} %project.8.after, bf16[512,4096]{1,0:T(8,128)(2,1)S(1)} %get-tuple-element.45.w_top, bf16[512,4096]{1,0:T(8,128)(2,1)S(1)} %get-tuple-element.46.w_low, bf16[384,1024]{1,0:T(8,128)(2,1)S(1)} %far_part.3.after.refs_0_.refs_1_), custom_call_target="tpu_custom_call" | custom-call | flops 8053063 | bytes 20971 | tf_op jit(solution)/shard_map/project/pallas_call | solution.py:391
  45.8 1.3 %project.10.after = bf16[512,1024]{1,0:T(8,128)(2,1)S(1)} custom-call(bf16[384,1024]{1,0:T(8,128)(2,1)S(1)} %project.9.after, bf16[512,4096]{1,0:T(8,128)(2,1)S(1)} %get-tuple-element.45.w_top, bf16[512,4096]{1,0:T(8,128)(2,1)S(1)} %get-tuple-element.46.w_low, bf16[128,1024]{1,0:T(8,128)(2,1)S(1)} %far_part.2.after.refs_0_, ...), custom_call_target="tpu_custom_call" | custom-call | flops 40000000000 | bytes 100000000 | tf_op jit(solution)/shard_map/project/pallas_call | solution.py:391
  48.0 0.7 %project.11.after = bf16[256,1024]{1,0:T(8,128)(2,1)S(1)} custom-call(bf16[512,1024]{1,0:T(8,128)(2,1)S(1)} %project.10.after, bf16[512,4096]{1,0:T(8,128)(2,1)S(1)} %get-tuple-element.45.w_top, bf16[512,4096]{1,0:T(8,128)(2,1)S(1)} %get-tuple-element.46.w_low, bf16[384,1024]{1,0:T(8,128)(2,1)S(1)} %far_part.3.after.refs_0_.refs_1_, ...), custom_call_target="tpu_custom_call" | custom-call | flops 40000000000 | bytes 100000000 | tf_op jit(solution)/shard_map/project/pallas_call | solution.py:391
  48.8 0.6 collective-permute-start.10
  49.8 1.6 %collective-permute-start.11 = (bf16[128,1024]{1,0:T(8,128)(2,1)S(1)}, bf16[128,1024]{1,0:T(8,128)(2,1)S(1)}, u32[]{:S(2)}, u32[]{:S(2)}) collective-permute-start(bf16[128,1024]{1,0:T(8,128)(2,1)S(1)} %project.12.after), channel_id=1, source_target_pairs={{0,2},{1,3},{2,0},{3,1},{4,6},{5,7},{6,4},{7,5},{8,10},{9,11},{10,... | collective-permute-start | bytes 786440 | tf_op jit(solution)/shard_map/ppermute | solution.py:487
  51.4 1.3 %project.13.own_ref = f32[512,1024]{1,0:T(8,128)S(1)} custom-call(bf16[128,1024]{1,0:T(8,128)(2,1)S(1)} %project.12.after, bf16[512,4096]{1,0:T(8,128)(2,1)S(1)} %get-tuple-element.45.w_top, bf16[512,4096]{1,0:T(8,128)(2,1)S(1)} %get-tuple-element.46.w_low, bf16[128,1024]{1,0:T(8,128)(2,1)S(1)} %far_part.2.after.refs_0_, ...), custom_call_target="tpu_custom_call" | custom-call | flops 10737418 | bytes 20971 | tf_op jit(solution)/shard_map/project/pallas_call | solution.py:391
  52.7 0.8 %finish.3.out_in = bf16[512,1024]{1,0:T(8,128)(2,1)} custom-call(f32[1,1024]{1,0:T(1,128)S(1)} %bitcast.3, f32[512,1024]{1,0:T(8,128)S(1)} %project.13.own_ref, bf16[512,1024]{1,0:T(8,128)(2,1)S(1)} %collective-permute-done.8.refs_0_, bf16[128,1024]{1,0:T(8,128)(2,1)S(1)} %collective-permute-done.9.refs_1_), custom_call_target="tpu_custom_call" | custom-call | flops 40000000000 | bytes 100000000 | tf_op jit(solution)/shard_map/finish/pallas_call | solution.py:413
  53.5 10.1 %collective-permute-done.10.refs_1_ = bf16[256,1024]{1,0:T(8,128)(2,1)S(1)} collective-permute-done((bf16[256,1024]{1,0:T(8,128)(2,1)S(1)}, bf16[256,1024]{1,0:T(8,128)(2,1)S(1)}, u32[]{:S(2)}, u32[]{:S(2)}) %collective-permute-start.10) | collective-permute-done | bytes 524320 | tf_op jit(solution)/shard_map/ppermute | solution.py:487
  63.6 0.9 %finish.4.out_in = bf16[512,1024]{1,0:T(8,128)(2,1)} custom-call(bf16[512,1024]{1,0:T(8,128)(2,1)} %finish.3.out_in, f32[512,1024]{1,0:T(8,128)S(1)} %project.13.own_ref, bf16[512,1024]{1,0:T(8,128)(2,1)S(1)} %collective-permute-done.8.refs_0_, bf16[256,1024]{1,0:T(8,128)(2,1)S(1)} %collective-permute-done.10.refs_1_), custom_call_target="tpu_custom_call", output_to_operand_aliasing={{}: (0, {})} | custom-call | flops 40000000000 | bytes 100000000 | tf_op jit(solution)/shard_map/finish/pallas_call | solution.py:413
  64.5 3.9 %collective-permute-done.11.refs_1_ = bf16[128,1024]{1,0:T(8,128)(2,1)S(1)} collective-permute-done((bf16[128,1024]{1,0:T(8,128)(2,1)S(1)}, bf16[128,1024]{1,0:T(8,128)(2,1)S(1)}, u32[]{:S(2)}, u32[]{:S(2)}) %collective-permute-start.11) | collective-permute-done | bytes 262176 | tf_op jit(solution)/shard_map/ppermute | solution.py:487
  68.4 0.8 %finish.5 = bf16[512,1024]{1,0:T(8,128)(2,1)} custom-call(bf16[512,1024]{1,0:T(8,128)(2,1)} %finish.4.out_in, f32[512,1024]{1,0:T(8,128)S(1)} %project.13.own_ref, bf16[512,1024]{1,0:T(8,128)(2,1)S(1)} %collective-permute-done.8.refs_0_, bf16[128,1024]{1,0:T(8,128)(2,1)S(1)} %collective-permute-done.11.refs_1_), custom_call_target="tpu_custom_call", output_to_operand_aliasing={{}: (0, {})} | custom-call | flops 40000000000 | bytes 100000000 | tf_op jit(solution)/shard_map/finish/pallas_call | solution.py:413
  (20 shorter events, 3.8 us)
Async XLA Ops:
  12.0 7.8 %collective-permute-start = (bf16[4,128,128]{2,1,0:T(8,128)(2,1)S(1)}, bf16[4,128,128]{2,1,0:T(8,128)(2,1)S(1)}, u32[]{:S(2)}, u32[]{:S(2)}) collective-permute-start(bf16[4,128,128]{2,1,0:T(8,128)(2,1)S(1)} %get-tuple-element.31), channel_id=1, source_target_pairs={{0,4},{4,0},{8,12},{12,8},{16,20},{20,16},{24,28},{28,24},{1,5},{5... | collective-permute-start | bytes 393224 | tf_op jit(solution)/shard_map/ppermute | solution.py:438
  19.8 5.9 %collective-permute-start.1 = (bf16[4,128,128]{2,1,0:T(8,128)(2,1)S(1)}, bf16[4,128,128]{2,1,0:T(8,128)(2,1)S(1)}, u32[]{:S(2)}, u32[]{:S(2)}) collective-permute-start(bf16[4,128,128]{2,1,0:T(8,128)(2,1)S(1)} %add_convert_fusion.1.after), channel_id=1, source_target_pairs={{0,8},{4,12},{8,0},{12,4},{16,24},{20,28},{24,16},{28,20},{1,9},{5... | collective-permute-start | bytes 393224 | tf_op jit(solution)/shard_map/ppermute | solution.py:438
  25.7 9.2 %collective-permute-start.4 = (bf16[4,128,128]{2,1,0:T(8,128)(2,1)S(1)}, bf16[4,128,128]{2,1,0:T(8,128)(2,1)S(1)}, u32[]{:S(2)}, u32[]{:S(2)}) collective-permute-start(bf16[4,128,128]{2,1,0:T(8,128)(2,1)S(1)} %add_convert_fusion.after), channel_id=1, source_target_pairs={{0,16},{4,20},{8,24},{12,28},{16,0},{20,4},{24,8},{28,12},{1,17},{... | collective-permute-start | bytes 393224 | tf_op jit(solution)/shard_map/ppermute | solution.py:438
  28.4 7.1 %collective-permute-start.2 = (bf16[4,128,128]{2,1,0:T(8,128)(2,1)S(1)}, bf16[4,128,128]{2,1,0:T(8,128)(2,1)S(1)}, u32[]{:S(2)}, u32[]{:S(2)}) collective-permute-start(bf16[4,128,128]{2,1,0:T(8,128)(2,1)S(1)} %get-tuple-element.42.after), channel_id=1, source_target_pairs={{0,4},{4,0},{8,12},{12,8},{16,20},{20,16},{24,28},{28,24},{1,5},{5... | collective-permute-start | bytes 393224 | tf_op jit(solution)/shard_map/ppermute | solution.py:438
  28.9 6.7 %collective-permute-start.3 = (bf16[4,128,128]{2,1,0:T(8,128)(2,1)S(1)}, bf16[4,128,128]{2,1,0:T(8,128)(2,1)S(1)}, u32[]{:S(2)}, u32[]{:S(2)}) collective-permute-start(bf16[4,128,128]{2,1,0:T(8,128)(2,1)S(1)} %collective-permute-done.1.refs_5_), channel_id=1, source_target_pairs={{0,4},{4,0},{8,12},{12,8},{16,20},{20,16},{24,28},{28,24},{1,5},{5... | collective-permute-start | bytes 393224 | tf_op jit(solution)/shard_map/ppermute | solution.py:438
  30.4 9.5 %copy-start = (f32[1024]{0:T(1024)S(1)}, f32[1024]{0:T(1024)}, u32[]{:S(2)}) copy-start(f32[1024]{0:T(1024)} %param.13) | copy-start | bytes 12292
  34.9 5.0 %collective-permute-start.5 = (bf16[4,128,128]{2,1,0:T(8,128)(2,1)S(1)}, bf16[4,128,128]{2,1,0:T(8,128)(2,1)S(1)}, u32[]{:S(2)}, u32[]{:S(2)}) collective-permute-start(bf16[4,128,128]{2,1,0:T(8,128)(2,1)S(1)} %collective-permute-done.4.refs_7_), channel_id=1, source_target_pairs={{0,4},{4,0},{8,12},{12,8},{16,20},{20,16},{24,28},{28,24},{1,5},{5... | collective-permute-start | bytes 393224 | tf_op jit(solution)/shard_map/ppermute | solution.py:438
  41.1 1.6 %collective-permute-start.6 = (bf16[128,1024]{1,0:T(8,128)(2,1)S(1)}, bf16[128,1024]{1,0:T(8,128)(2,1)S(1)}, u32[]{:S(2)}, u32[]{:S(2)}) collective-permute-start(bf16[128,1024]{1,0:T(8,128)(2,1)S(1)} %project.7.after), channel_id=1, source_target_pairs={{0,1},{1,0},{2,3},{3,2},{4,5},{5,4},{6,7},{7,6},{8,9},{9,8},{10,11... | collective-permute-start | bytes 786440 | tf_op jit(solution)/shard_map/ppermute | solution.py:478
  43.1 9.5 %collective-permute-start.9 = (bf16[128,1024]{1,0:T(8,128)(2,1)S(1)}, bf16[128,1024]{1,0:T(8,128)(2,1)S(1)}, u32[]{:S(2)}, u32[]{:S(2)}) collective-permute-start(bf16[128,1024]{1,0:T(8,128)(2,1)S(1)} %project.8.after), channel_id=1, source_target_pairs={{0,2},{1,3},{2,0},{3,1},{4,6},{5,7},{6,4},{7,5},{8,10},{9,11},{10,... | collective-permute-start | bytes 786440 | tf_op jit(solution)/shard_map/ppermute | solution.py:487
  45.7 2.4 %collective-permute-start.7 = (bf16[384,1024]{1,0:T(8,128)(2,1)S(1)}, bf16[384,1024]{1,0:T(8,128)(2,1)S(1)}, u32[]{:S(2)}, u32[]{:S(2)}) collective-permute-start(bf16[384,1024]{1,0:T(8,128)(2,1)S(1)} %project.9.after), channel_id=1, source_target_pairs={{0,1},{1,0},{2,3},{3,2},{4,5},{5,4},{6,7},{7,6},{8,9},{9,8},{10,11... | collective-permute-start | bytes 2359304 | tf_op jit(solution)/shard_map/ppermute | solution.py:478
  47.0 5.6 %collective-permute-start.8 = (bf16[512,1024]{1,0:T(8,128)(2,1)S(1)}, bf16[512,1024]{1,0:T(8,128)(2,1)S(1)}, u32[]{:S(2)}, u32[]{:S(2)}) collective-permute-start(bf16[512,1024]{1,0:T(8,128)(2,1)S(1)} %project.10.after), channel_id=1, source_target_pairs={{0,1},{1,0},{2,3},{3,2},{4,5},{5,4},{6,7},{7,6},{8,9},{9,8},{10,11... | collective-permute-start | bytes 3145736 | tf_op jit(solution)/shard_map/ppermute | solution.py:497
  48.8 14.8 %collective-permute-start.10 = (bf16[256,1024]{1,0:T(8,128)(2,1)S(1)}, bf16[256,1024]{1,0:T(8,128)(2,1)S(1)}, u32[]{:S(2)}, u32[]{:S(2)}) collective-permute-start(bf16[256,1024]{1,0:T(8,128)(2,1)S(1)} %project.11.after), channel_id=1, source_target_pairs={{0,2},{1,3},{2,0},{3,1},{4,6},{5,7},{6,4},{7,5},{8,10},{9,11},{10,... | collective-permute-start | bytes 1572872 | tf_op jit(solution)/shard_map/ppermute | solution.py:487
  49.8 18.6 %collective-permute-start.11 = (bf16[128,1024]{1,0:T(8,128)(2,1)S(1)}, bf16[128,1024]{1,0:T(8,128)(2,1)S(1)}, u32[]{:S(2)}, u32[]{:S(2)}) collective-permute-start(bf16[128,1024]{1,0:T(8,128)(2,1)S(1)} %project.12.after), channel_id=1, source_target_pairs={{0,2},{1,3},{2,0},{3,1},{4,6},{5,7},{6,4},{7,5},{8,10},{9,11},{10,... | collective-permute-start | bytes 786440 | tf_op jit(solution)/shard_map/ppermute | solution.py:487

commit v2 on v1

--- a/solution.py
+++ b/solution.py
@@ -52,8 +52,7 @@
     x_in = [pltpu.make_async_copy(x_hbm.at[:, a], x.at[:, a], sem.at[0, c]) for c, a in enumerate(at)]
     v_in = [pltpu.make_async_copy(wv_hbm.at[a], wv.at[a], sem.at[1, c]) for c, a in enumerate(at)]
     k_in = [pltpu.make_async_copy(wk_hbm.at[a], wk.at[a], sem.at[2, c]) for c, a in enumerate(at)]
-    first_half = pl.ds(0, size // 2)
-    q_in = [pltpu.make_async_copy(wq_hbm.at[a, first_half], wq.at[a], sem.at[3, c]) for c, a in enumerate(at)]
+    q_in = [pltpu.make_async_copy(wq_hbm.at[a], wq.at[a], sem.at[3, c]) for c, a in enumerate(at)]
     for c in range(cuts):
         starts((x_in[c], v_in[c]))
     starts(k_in)
@@ -97,7 +96,7 @@
         out_specs=[VMEM] * 6,
         out_shape=[
             pltpu.VMEM((rows, depth), bf16),
-            pltpu.VMEM((depth, size // 2), bf16),
+            pltpu.VMEM((depth, size), bf16),
             pltpu.VMEM((rows, size), bf16),
             pltpu.VMEM((size, rows), bf16),
             part,
@@ -188,54 +187,52 @@
     ]
 
 
-def query_product(x, wq, raw_ref, meanwhile):
+def query_product(x, wq, raw_ref, first, meanwhile):
     rows, depth = x.shape
+    size = raw_ref.shape[1]
     cuts = 8
     cut = depth // cuts
     for c in range(cuts):
         a = slice(c * cut, (c + 1) * cut)
-        term = mm(x[:, a], wq[a, :])
+        term = mm(x[:, a], wq[a, first : first + size])
         raw_ref[...] = term if c == 0 else raw_ref[...] + term
         meanwhile(c, cuts)
 
 
-def queries_first_body(x, wq, wq_hbm, lam_hbm, prior_hbm, after, raw_ref, wq_next, lam, prior, sem):
-    depth, size = wq.shape
-    cut = depth // 8
+def queries_first_body(x, wq, lam_hbm, prior_hbm, after, raw_ref, lam, prior, sem):
     copies = [pltpu.make_async_copy(lam_hbm, lam, sem.at[0])]
-    for c in range(8):
-        a = pl.ds(c * cut, cut)
-        copies.append(pltpu.make_async_copy(wq_hbm.at[a, pl.ds(size, size)], wq_next.at[a], sem.at[1 + c]))
+    heads = prior.shape[1]
     for p in range(prior.shape[0]):
-        copies.append(pltpu.make_async_copy(prior_hbm.at[p], prior.at[p], sem.at[9 + p]))
+        for h in range(heads):
+            copies.append(pltpu.make_async_copy(prior_hbm.at[p, h], prior.at[p, h], sem.at[1 + p * heads + h]))
     starts(copies)
-    query_product(x, wq, raw_ref, lambda c, cuts: None)
+    query_product(x, wq, raw_ref, 0, lambda c, cuts: None)
     for copy in copies:
         copy.wait()
 
 
-def queries_first(tokens, half_query, w_query, level_weights, prior_states, after):
+def queries_first(tokens, w_query, level_weights, prior_states, after):
     rows, depth = tokens.shape
-    size = half_query.shape[1]
+    size = w_query.shape[1] // 2
+    priors, heads = prior_states.shape[:2]
     return pl.pallas_call(
         queries_first_body,
-        in_specs=[VMEM, VMEM, HBM, HBM, HBM, ANY],
-        out_specs=[VMEM] * 4,
+        in_specs=[VMEM, VMEM, HBM, HBM, ANY],
+        out_specs=[VMEM] * 3,
         out_shape=[
             pltpu.VMEM((rows, size), f32),
-            pltpu.VMEM(half_query.shape, bf16),
             pltpu.VMEM(level_weights.shape, f32),
             pltpu.VMEM(prior_states.shape, f32),
         ],
-        scratch_shapes=[pltpu.SemaphoreType.DMA((9 + prior_states.shape[0],))],
+        scratch_shapes=[pltpu.SemaphoreType.DMA((1 + priors * heads,))],
         compiler_params=params(16),
         cost_estimate=cost(2 * rows * depth * size, 2 * (rows * depth + depth * size)),
         name="queries_first",
-    )(tokens, half_query, in_hbm(w_query), in_hbm(level_weights), in_hbm(prior_states), after)
+    )(tokens, w_query, in_hbm(level_weights), in_hbm(prior_states), after)
 
 
 def queries_second_body(width, x, wq, raw_old, w_hbm, after, qt_ref, raw_ref, w_ref, sem):
-    copies = row_copies(w_hbm, 0, w_ref, sem, 0, 8)
+    copies = row_copies(w_hbm, 0, w_ref, sem, 0, sem.shape[0])
     starts(copies)
     heads = raw_old.shape[1] // width
 
@@ -244,14 +241,14 @@
             own = slice(h * width, (h + 1) * width)
             leave_tiles(qt_ref, own, finished(raw_old[:, own]))
 
-    query_product(x, wq, raw_ref, meanwhile)
+    query_product(x, wq, raw_ref, raw_old.shape[1], meanwhile)
     for copy in copies:
         copy.wait()
 
 
-def queries_second(tokens, half_query, raw_old, w_out, after, width):
+def queries_second(tokens, w_query, raw_old, w_out, after, width):
     rows, depth = tokens.shape
-    size = half_query.shape[1]
+    size = w_query.shape[1] // 2
     return pl.pallas_call(
         functools.partial(queries_second_body, width),
         in_specs=[VMEM, VMEM, VMEM, HBM, ANY],
@@ -261,16 +258,14 @@
             pltpu.VMEM((rows, size), f32),
             pltpu.VMEM((w_out.shape[0] // 2, w_out.shape[1]), bf16),
         ],
-        scratch_shapes=[pltpu.SemaphoreType.DMA((8,))],
+        scratch_shapes=[pltpu.SemaphoreType.DMA((w_out.shape[0] // 32,))],
         compiler_params=params(16),
         cost_estimate=cost(2 * rows * depth * size, 2 * (rows * depth + depth * size)),
         name="queries_second",
-    )(tokens, half_query, raw_old, in_hbm(w_out), after)
-
-
-def attention_body(width, lam_ref, prior_ref, w_hbm, after, qt_old, raw, k_ref, vt_ref, acc_ref, qt_ref, w_ref, sem):
-    copies = row_copies(w_hbm, w_ref.shape[0], w_ref, sem, 0, 8)
-    starts(copies)
+    )(tokens, w_query, raw_old, in_hbm(w_out), after)
+
+
+def attention_body(width, lam_ref, prior_ref, after, qt_old, raw, k_ref, vt_ref, acc_ref, qt_ref):
     heads = prior_ref.shape[1]
     per = heads // 2
     for h in range(heads):
@@ -285,26 +280,41 @@
         pieces = attend(qt, k_ref[:, every], vt_ref[every, :], lam_ref[:, h, :], prior)
         for i, piece in enumerate(pieces):
             acc_ref[i, every, :] = piece
-    for copy in copies:
-        copy.wait()
-
-
-def attention(qt_old, raw, keys, values_t, level_weights, prior_states, w_out, after, width):
+
+
+def attention(qt_old, raw, keys, values_t, level_weights, prior_states, after, width):
     tiles, size, take = qt_old.shape
     return pl.pallas_call(
         functools.partial(attention_body, width),
-        in_specs=[VMEM] * 2 + [HBM, ANY] + [VMEM] * 4,
-        out_specs=[VMEM] * 3,
-        out_shape=[
-            pltpu.VMEM((tiles, 2 * size, take), f32),
-            pltpu.VMEM(qt_old.shape, bf16),
-            pltpu.VMEM((w_out.shape[0] // 2, w_out.shape[1]), bf16),
-        ],
-        scratch_shapes=[pltpu.SemaphoreType.DMA((8,))],
+        in_specs=[VMEM] * 2 + [ANY] + [VMEM] * 4,
+        out_specs=[VMEM] * 2,
+        out_shape=[pltpu.VMEM((tiles, 2 * size, take), f32), pltpu.VMEM(qt_old.shape, bf16)],
         compiler_params=params(16),
         cost_estimate=FAR_APART,
         name="attention",
-    )(level_weights, prior_states, in_hbm(w_out), after, qt_old, raw, keys, values_t)
+    )(level_weights, prior_states, after, qt_old, raw, keys, values_t)
+
+
+def fetch_body(w_hbm, *refs):
+    w_ref, sem = refs[-2:]
+    copies = row_copies(w_hbm, w_ref.shape[0], w_ref, sem, 0, sem.shape[0])
+    starts(copies)
+    for copy in copies:
+        copy.wait()
+
+
+def fetch(w_out, after):
+    depth, total = w_out.shape
+    return pl.pallas_call(
+        fetch_body,
+        in_specs=[HBM] + [ANY] * len(after),
+        out_specs=VMEM,
+        out_shape=pltpu.VMEM((depth // 2, total), bf16),
+        scratch_shapes=[pltpu.SemaphoreType.DMA((depth // 32,))],
+        compiler_params=params(4),
+        cost_estimate=cost(0, 2 * depth * total),
+        name="fetch",
+    )(in_hbm(w_out), *after)
 
 
 def far_body(width, first_level, halves, counts, first, number, after, *refs):
@@ -443,30 +453,26 @@
     def not_before(value, done):
         return lax.optimization_barrier((value, done))[0]
 
-    tokens, half_query, keys, values_t, keep, give = keys_values(tokens, w_key, w_value, w_query, width)
+    tokens, w_query, keys, values_t, keep, give = keys_values(tokens, w_key, w_value, w_query, width)
     got = send(give, 0)
-    raw_a, next_query, level_weights, prior_states = queries_first(
-        tokens, half_query, w_query, level_weights, prior_states, keep
-    )
+    raw_a, level_weights, prior_states = queries_first(tokens, w_query, level_weights, prior_states, keep)
     got = not_before(got, raw_a)
     running = merge(keep, got)
     kept, swapped = [[got]], []
     for j in range(1, nbits):
-        cut = running.shape[0]
-        gots = [send(running[n : n + cut], j) for n in range(0, running.shape[0], cut)]
+        gots = [send(running, j)]
         if j == 1:
-            q_a, done, w_top = queries_second(tokens, next_query, raw_a, w_out, running, width)
+            q_a, done, w_top = queries_second(tokens, w_query, raw_a, w_out, running, width)
         if j == nbits - 1:
-            acc, q_b, w_low = attention(
-                q_a, done, keys, values_t, level_weights, prior_states, w_out, running, width
-            )
+            acc, q_b = attention(q_a, done, keys, values_t, level_weights, prior_states, running, width)
             swapped = [[send(not_before(keep, running), 0)]] + [[send(not_before(old[0], running), 0)] for old in kept[1:]]
             done = acc
         gots = [not_before(got, done) for got in gots]
         if j < nbits - 1:
             running = merge(running, gots[0])
         kept.append(gots)
-    swapped.append([send(got, 0) for got in kept[-1]])
+    w_low = fetch(w_out, [pieces[0] for pieces in kept[-1:] + swapped])
+    swapped.append([not_before(send(got, 0), w_low) for got in kept[-1]])
     states = [pieces for pair in zip(kept, swapped) for pieces in pair]
     queries_t = [q_a, q_b]
     weights = (w_top, w_low)

time: 69.3 us -> 67.9 us (0.980)
  waiting for transfers between devices: 19.5 us -> 17.6 us
    pallas_call x1, Pallas kernels: 4.46 us -> 2.58 us  [attention(): pl.pallas_call(functools.partial(attention_body, width), in_specs=[VMEM]...]
    ppermute x6, waiting for transfers between devices: 4.48 us -> 2.65 us  [send(): return lax.ppermute(state, 'seq', [(r, r ^ 1 << j) for r in range(count)])]
    pallas_call x1 -> x2, Pallas kernels: 4.74 us -> 6.36 us  [the longest x1 3.68 us: queries_first(): pl.pallas_call(queries_first_body, in_specs=[VMEM, VMEM, HBM, HBM, ANY],...]
  transfers between devices with their start and end apart: 12 -> 12, of which waited for: 6 -> 7; matrix products, arithmetic and copies ran while one was open for 0% -> 0% of each run, Pallas kernels for 30% -> 31%
where the time goes in v2:
time: 67.9 us; the launch traced here: 67.7 us
  Pallas kernels  35.1 us (52%)
  waiting for transfers between devices  17.6 us (26%)
  starting transfers between devices  14.7 us (22%)
    ppermute x3, waiting for transfers between devices, onward(): lax.ppermute(after, 'head', [(i, (i + 2 * d) % groups) for i in range(gro...  14 us
    pallas_call x1, Pallas kernels, keys_values(): pl.pallas_call(functools.partial(keys_values_body, width), in_specs=[HBM]...  11.9 us
    ppermute x6, starting transfers between devices, send(): return lax.ppermute(state, 'seq', [(r, r ^ 1 << j) for r in range(count)])  10.3 us
    pallas_call x7, Pallas kernels, project(): pl.pallas_call(functools.partial(project_body, flip, d, groups, start, ta...  5.66 us
    pallas_call x1, Pallas kernels, queries_second(): pl.pallas_call(functools.partial(queries_second_body, width), in_specs=[V...  4.59 us
    ppermute x3, starting transfers between devices, onward(): lax.ppermute(after, 'head', [(i, (i + 2 * d) % groups) for i in range(gro...  3.69 us
    pallas_call x1, Pallas kernels, queries_first(): pl.pallas_call(queries_first_body, in_specs=[VMEM, VMEM, HBM, HBM, ANY],...  3.68 us
    pallas_call x1, Pallas kernels, fetch(): pl.pallas_call(fetch_body, in_specs=[HBM] + [ANY] * len(after), out_specs...  2.68 us
  transfers between devices with their start and end apart: 12, of which 7 were waited for; matrix products, arithmetic and copies ran while one was open for 0% of the time, Pallas kernels for 31%

profile of v2, /device:TPU:0, one launch (start us, length us, event | category | flops | bytes accessed | tf_op | source)
XLA Modules:
  0.0 67.7 jit_solution(7099340951798517634)
XLA Ops:
  0.0 11.9 %keys_values.1 = (bf16[512,4096]{1,0:T(8,128)(2,1)S(1)}, bf16[4096,1024]{1,0:T(8,128)(2,1)S(1)}, bf16[512,1024]{1,0:T(8,128)(2,1)S(1)}, bf16[1024,512]{1,0:T(8,1...) custom-call(bf16[512,4096]{1,0:T(8,128)(2,1)} %x_hbm.1, bf16[4096,1024]{1,0:T(8,128)(2,1)} %wk_hbm.1, ...), custom_call_target="tpu_custom_call" | custom-call | flops 85899344 | bytes 209715 | tf_op jit(solution)/shard_map/keys_values/pallas_call | solution.py:93
  12.0 3.0 %collective-permute-start = (bf16[4,128,128]{2,1,0:T(8,128)(2,1)S(1)}, bf16[4,128,128]{2,1,0:T(8,128)(2,1)S(1)}, u32[]{:S(2)}, u32[]{:S(2)}) collective-permute-start(bf16[4,128,128]{2,1,0:T(8,128)(2,1)S(1)} %get-tuple-element.30), channel_id=1, source_target_pairs={{0,4},{4,0},{8,12},{12,8},{16,20},{20,16},{24,28},{28,24},{1,5},{5... | collective-permute-start | bytes 393224 | tf_op jit(solution)/shard_map/ppermute | solution.py:448
  15.0 3.7 %queries_first.1 = (f32[512,512]{1,0:T(8,128)S(1)}, f32[21,8,512]{2,1,0:T(8,128)S(1)}, f32[4,8,128,128]{3,2,1,0:T(8,128)S(1)}) custom-call(bf16[512,4096]{1,0:T(8,128)(2,1)S(1)} %get-tuple-element.25.x, bf16[4096,1024]{1,0:T(8,128)(2,1)S(1)} %get-tuple-element.26.wq, f32[21,8,512]{2,1,0:T(8,128)} %lam_hbm.1, f32[4,8,128,128]{3,2,1,0:T(8,128)} %prior_hbm.1, ...), custom_call_target="tpu_custom_call" | custom-call | flops 21474836 | bytes 83886 | tf_op jit(solution)/shard_map/queries_first/pallas_call | solution.py:218
  18.7 1.7 %collective-permute-start.1 = (bf16[4,128,128]{2,1,0:T(8,128)(2,1)S(1)}, bf16[4,128,128]{2,1,0:T(8,128)(2,1)S(1)}, u32[]{:S(2)}, u32[]{:S(2)}) collective-permute-start(bf16[4,128,128]{2,1,0:T(8,128)(2,1)S(1)} %add_convert_fusion.1.after), channel_id=1, source_target_pairs={{0,8},{4,12},{8,0},{12,4},{16,24},{20,28},{24,16},{28,20},{1,9},{5... | collective-permute-start | bytes 393224 | tf_op jit(solution)/shard_map/ppermute | solution.py:448
  20.4 4.6 %queries_second.1 = (bf16[4,512,128]{2,1,0:T(8,128)(2,1)S(1)}, f32[512,512]{1,0:T(8,128)S(1)}, bf16[512,4096]{1,0:T(8,128)(2,1)S(1)}) custom-call(bf16[512,4096]{1,0:T(8,128)(2,1)S(1)} %get-tuple-element.25.x, bf16[4096,1024]{1,0:T(8,128)(2,1)S(1)} %get-tuple-element.26.wq, f32[512,512]{1,0:T(8,128)S(1)} %get-tuple-element.31.raw_old, ...), custom_call_target="tpu_custom_call" | custom-call | flops 21474836 | bytes 83886 | tf_op jit(solution)/shard_map/queries_second/pallas_call | solution.py:252
  25.0 2.7 %collective-permute-start.4 = (bf16[4,128,128]{2,1,0:T(8,128)(2,1)S(1)}, bf16[4,128,128]{2,1,0:T(8,128)(2,1)S(1)}, u32[]{:S(2)}, u32[]{:S(2)}) collective-permute-start(bf16[4,128,128]{2,1,0:T(8,128)(2,1)S(1)} %add_convert_fusion.after), channel_id=1, source_target_pairs={{0,16},{4,20},{8,24},{12,28},{16,0},{20,4},{24,8},{28,12},{1,17},{... | collective-permute-start | bytes 393224 | tf_op jit(solution)/shard_map/ppermute | solution.py:448
  27.7 1.5 %collective-permute-start.2 = (bf16[4,128,128]{2,1,0:T(8,128)(2,1)S(1)}, bf16[4,128,128]{2,1,0:T(8,128)(2,1)S(1)}, u32[]{:S(2)}, u32[]{:S(2)}) collective-permute-start(bf16[4,128,128]{2,1,0:T(8,128)(2,1)S(1)} %get-tuple-element.40.after), channel_id=1, source_target_pairs={{0,4},{4,0},{8,12},{12,8},{16,20},{20,16},{24,28},{28,24},{1,5},{5... | collective-permute-start | bytes 393224 | tf_op jit(solution)/shard_map/ppermute | solution.py:448
  29.7 2.6 %attention.1 = (f32[4,1024,128]{2,1,0:T(8,128)S(1)}, bf16[4,512,128]{2,1,0:T(8,128)(2,1)S(1)}) custom-call(f32[21,8,512]{2,1,0:T(8,128)S(1)} %get-tuple-element.28.lam_ref.refs_9_, f32[4,8,128,128]{3,2,1,0:T(8,128)S(1)} %get-tuple-element.29.prior_ref, bf16[4,128,128]{2,1,0:T(8,128)(2,1)S(1)} %add_convert_fusion.after, ...), custom_call_target="tpu_custom_call" | custom-call | flops 40000000000 | bytes 100000000 | tf_op jit(solution)/shard_map/attention/pallas_call | solution.py:287
  32.3 1.1 %collective-permute-done.4.refs_0_.refs_7_ = bf16[4,128,128]{2,1,0:T(8,128)(2,1)S(1)} collective-permute-done((bf16[4,128,128]{2,1,0:T(8,128)(2,1)S(1)}, bf16[4,128,128]{2,1,0:T(8,128)(2,1)S(1)}, u32[]{:S(2)}, u32[]{:S(2)}) %collective-permute-start.4) | collective-permute-done | bytes 131104 | tf_op jit(solution)/shard_map/ppermute | solution.py:448
  33.4 0.9 %collective-permute-start.5 = (bf16[4,128,128]{2,1,0:T(8,128)(2,1)S(1)}, bf16[4,128,128]{2,1,0:T(8,128)(2,1)S(1)}, u32[]{:S(2)}, u32[]{:S(2)}) collective-permute-start(bf16[4,128,128]{2,1,0:T(8,128)(2,1)S(1)} %collective-permute-done.4.refs_0_.refs_7_), channel_id=1, source_target_pairs={{0,4},{4,0},{8,12},{12,8},{16,20},{20,16},{24,28},{28,24},{1,5},{5... | collective-permute-start | bytes 393224 | tf_op jit(solution)/shard_map/ppermute | solution.py:448
  34.9 2.7 %fetch.1.w_low = bf16[512,4096]{1,0:T(8,128)(2,1)S(1)} custom-call(bf16[1024,4096]{1,0:T(8,128)(2,1)} %w_hbm.3, bf16[4,128,128]{2,1,0:T(8,128)(2,1)S(1)} %collective-permute-done.4.refs_0_.refs_7_, bf16[4,128,128]{2,1,0:T(8,128)(2,1)S(1)} %collective-permute-done.2.refs_1_.refs_4_, bf16[4,128,128]{2,1,0:T(8,128)(2,1)S(1)} %collective-permute-done.3.refs_2_.refs_6_), custom_call_target="tpu_custom_call" | custom-call | bytes 83886 | tf_op jit(solution)/shard_map/fetch/pallas_call | solution.py:308
  37.6 1.0 %collective-permute-done.5.refs_8_ = bf16[4,128,128]{2,1,0:T(8,128)(2,1)S(1)} collective-permute-done((bf16[4,128,128]{2,1,0:T(8,128)(2,1)S(1)}, bf16[4,128,128]{2,1,0:T(8,128)(2,1)S(1)}, u32[]{:S(2)}, u32[]{:S(2)}) %collective-permute-start.5) | collective-permute-done | bytes 131104 | tf_op jit(solution)/shard_map/ppermute | solution.py:448
  39.7 1.0 %far_part.3.after.refs_0_.refs_1_ = bf16[384,1024]{1,0:T(8,128)(2,1)S(1)} custom-call(bf16[128,1024]{1,0:T(8,128)(2,1)S(1)} %project.7.after, bf16[4,512,128]{2,1,0:T(8,128)(2,1)S(1)} %get-tuple-element.35.qt_old.refs_0_, bf16[4,512,128]{2,1,0:T(8,128)(2,1)S(1)} %get-tuple-element.39.refs_1_, f32[4,1024,128]{2,1,0:T(8,128)S(1)} %get-tuple-element.38.after.refs_2_, ...), custom_call_target="tpu_custom_call" | custom-call | flops 5368709 | bytes 41943 | tf_op jit(solution)/shard_map/far_part/pallas_call | solution.py:366
  41.7 1.5 %collective-permute-start.9 = (bf16[128,1024]{1,0:T(8,128)(2,1)S(1)}, bf16[128,1024]{1,0:T(8,128)(2,1)S(1)}, u32[]{:S(2)}, u32[]{:S(2)}) collective-permute-start(bf16[128,1024]{1,0:T(8,128)(2,1)S(1)} %project.8.after), channel_id=1, source_target_pairs={{0,2},{1,3},{2,0},{3,1},{4,6},{5,7},{6,4},{7,5},{8,10},{9,11},{10,... | collective-permute-start | bytes 786440 | tf_op jit(solution)/shard_map/ppermute | solution.py:493
  43.2 1.0 %project.9.after = bf16[384,1024]{1,0:T(8,128)(2,1)S(1)} custom-call(bf16[128,1024]{1,0:T(8,128)(2,1)S(1)} %project.8.after, bf16[512,4096]{1,0:T(8,128)(2,1)S(1)} %get-tuple-element.44.w_top, bf16[512,4096]{1,0:T(8,128)(2,1)S(1)} %fetch.1.w_low, bf16[384,1024]{1,0:T(8,128)(2,1)S(1)} %far_part.3.after.refs_0_.refs_1_), custom_call_target="tpu_custom_call" | custom-call | flops 8053063 | bytes 20971 | tf_op jit(solution)/shard_map/project/pallas_call | solution.py:401
  44.3 1.3 %project.10.after = bf16[512,1024]{1,0:T(8,128)(2,1)S(1)} custom-call(bf16[384,1024]{1,0:T(8,128)(2,1)S(1)} %project.9.after, bf16[512,4096]{1,0:T(8,128)(2,1)S(1)} %get-tuple-element.44.w_top, bf16[512,4096]{1,0:T(8,128)(2,1)S(1)} %fetch.1.w_low, bf16[128,1024]{1,0:T(8,128)(2,1)S(1)} %far_part.2.after.refs_0_, ...), custom_call_target="tpu_custom_call" | custom-call | flops 40000000000 | bytes 100000000 | tf_op jit(solution)/shard_map/project/pallas_call | solution.py:401
  46.5 0.7 %project.11.after = bf16[256,1024]{1,0:T(8,128)(2,1)S(1)} custom-call(bf16[512,1024]{1,0:T(8,128)(2,1)S(1)} %project.10.after, bf16[512,4096]{1,0:T(8,128)(2,1)S(1)} %get-tuple-element.44.w_top, bf16[512,4096]{1,0:T(8,128)(2,1)S(1)} %fetch.1.w_low, bf16[384,1024]{1,0:T(8,128)(2,1)S(1)} %far_part.3.after.refs_0_.refs_1_, ...), custom_call_target="tpu_custom_call" | custom-call | flops 40000000000 | bytes 100000000 | tf_op jit(solution)/shard_map/project/pallas_call | solution.py:401
  48.4 1.5 %collective-permute-start.11 = (bf16[128,1024]{1,0:T(8,128)(2,1)S(1)}, bf16[128,1024]{1,0:T(8,128)(2,1)S(1)}, u32[]{:S(2)}, u32[]{:S(2)}) collective-permute-start(bf16[128,1024]{1,0:T(8,128)(2,1)S(1)} %project.12.after), channel_id=1, source_target_pairs={{0,2},{1,3},{2,0},{3,1},{4,6},{5,7},{6,4},{7,5},{8,10},{9,11},{10,... | collective-permute-start | bytes 786440 | tf_op jit(solution)/shard_map/ppermute | solution.py:493
  49.9 1.3 %project.13.own_ref = f32[512,1024]{1,0:T(8,128)S(1)} custom-call(bf16[128,1024]{1,0:T(8,128)(2,1)S(1)} %project.12.after, bf16[512,4096]{1,0:T(8,128)(2,1)S(1)} %get-tuple-element.44.w_top, bf16[512,4096]{1,0:T(8,128)(2,1)S(1)} %fetch.1.w_low, bf16[128,1024]{1,0:T(8,128)(2,1)S(1)} %far_part.2.after.refs_0_, bf16[384,1024]{1,0:T(8,128)(2,1)S(1)} %far_part.3.after.refs_0_.refs_1_), custom_call_target="tpu_custom_call" | custom-call | flops 10737418 | bytes 20971 | tf_op jit(solution)/shard_map/project/pallas_call | solution.py:401
  51.2 0.8 %finish.3.out_in = bf16[512,1024]{1,0:T(8,128)(2,1)} custom-call(f32[1,1024]{1,0:T(1,128)S(1)} %bitcast.3, f32[512,1024]{1,0:T(8,128)S(1)} %project.13.own_ref, bf16[512,1024]{1,0:T(8,128)(2,1)S(1)} %collective-permute-done.8.refs_0_, bf16[128,1024]{1,0:T(8,128)(2,1)S(1)} %collective-permute-done.9.refs_1_), custom_call_target="tpu_custom_call" | custom-call | flops 40000000000 | bytes 100000000 | tf_op jit(solution)/shard_map/finish/pallas_call | solution.py:423
  52.0 10.1 %collective-permute-done.10.refs_1_ = bf16[256,1024]{1,0:T(8,128)(2,1)S(1)} collective-permute-done((bf16[256,1024]{1,0:T(8,128)(2,1)S(1)}, bf16[256,1024]{1,0:T(8,128)(2,1)S(1)}, u32[]{:S(2)}, u32[]{:S(2)}) %collective-permute-start.10) | collective-permute-done | bytes 524320 | tf_op jit(solution)/shard_map/ppermute | solution.py:493
  62.1 0.9 %finish.4.out_in = bf16[512,1024]{1,0:T(8,128)(2,1)} custom-call(bf16[512,1024]{1,0:T(8,128)(2,1)} %finish.3.out_in, f32[512,1024]{1,0:T(8,128)S(1)} %project.13.own_ref, bf16[512,1024]{1,0:T(8,128)(2,1)S(1)} %collective-permute-done.8.refs_0_, bf16[256,1024]{1,0:T(8,128)(2,1)S(1)} %collective-permute-done.10.refs_1_), custom_call_target="tpu_custom_call", output_to_operand_aliasing={{}: (0, {})} | custom-call | flops 40000000000 | bytes 100000000 | tf_op jit(solution)/shard_map/finish/pallas_call | solution.py:423
  63.0 3.9 %collective-permute-done.11.refs_1_ = bf16[128,1024]{1,0:T(8,128)(2,1)S(1)} collective-permute-done((bf16[128,1024]{1,0:T(8,128)(2,1)S(1)}, bf16[128,1024]{1,0:T(8,128)(2,1)S(1)}, u32[]{:S(2)}, u32[]{:S(2)}) %collective-permute-start.11) | collective-permute-done | bytes 262176 | tf_op jit(solution)/shard_map/ppermute | solution.py:493
  66.9 0.8 %finish.5 = bf16[512,1024]{1,0:T(8,128)(2,1)} custom-call(bf16[512,1024]{1,0:T(8,128)(2,1)} %finish.4.out_in, f32[512,1024]{1,0:T(8,128)S(1)} %project.13.own_ref, bf16[512,1024]{1,0:T(8,128)(2,1)S(1)} %collective-permute-done.8.refs_0_, bf16[128,1024]{1,0:T(8,128)(2,1)S(1)} %collective-permute-done.11.refs_1_), custom_call_target="tpu_custom_call", output_to_operand_aliasing={{}: (0, {})} | custom-call | flops 40000000000 | bytes 100000000 | tf_op jit(solution)/shard_map/finish/pallas_call | solution.py:423
  (21 shorter events, 5.3 us)
Async XLA Ops:
  12.0 6.7 %collective-permute-start = (bf16[4,128,128]{2,1,0:T(8,128)(2,1)S(1)}, bf16[4,128,128]{2,1,0:T(8,128)(2,1)S(1)}, u32[]{:S(2)}, u32[]{:S(2)}) collective-permute-start(bf16[4,128,128]{2,1,0:T(8,128)(2,1)S(1)} %get-tuple-element.30), channel_id=1, source_target_pairs={{0,4},{4,0},{8,12},{12,8},{16,20},{20,16},{24,28},{28,24},{1,5},{5... | collective-permute-start | bytes 393224 | tf_op jit(solution)/shard_map/ppermute | solution.py:448
  18.7 6.3 %collective-permute-start.1 = (bf16[4,128,128]{2,1,0:T(8,128)(2,1)S(1)}, bf16[4,128,128]{2,1,0:T(8,128)(2,1)S(1)}, u32[]{:S(2)}, u32[]{:S(2)}) collective-permute-start(bf16[4,128,128]{2,1,0:T(8,128)(2,1)S(1)} %add_convert_fusion.1.after), channel_id=1, source_target_pairs={{0,8},{4,12},{8,0},{12,4},{16,24},{20,28},{24,16},{28,20},{1,9},{5... | collective-permute-start | bytes 393224 | tf_op jit(solution)/shard_map/ppermute | solution.py:448
  25.0 8.3 %collective-permute-start.4 = (bf16[4,128,128]{2,1,0:T(8,128)(2,1)S(1)}, bf16[4,128,128]{2,1,0:T(8,128)(2,1)S(1)}, u32[]{:S(2)}, u32[]{:S(2)}) collective-permute-start(bf16[4,128,128]{2,1,0:T(8,128)(2,1)S(1)} %add_convert_fusion.after), channel_id=1, source_target_pairs={{0,16},{4,20},{8,24},{12,28},{16,0},{20,4},{24,8},{28,12},{1,17},{... | collective-permute-start | bytes 393224 | tf_op jit(solution)/shard_map/ppermute | solution.py:448
  27.7 6.6 %collective-permute-start.2 = (bf16[4,128,128]{2,1,0:T(8,128)(2,1)S(1)}, bf16[4,128,128]{2,1,0:T(8,128)(2,1)S(1)}, u32[]{:S(2)}, u32[]{:S(2)}) collective-permute-start(bf16[4,128,128]{2,1,0:T(8,128)(2,1)S(1)} %get-tuple-element.40.after), channel_id=1, source_target_pairs={{0,4},{4,0},{8,12},{12,8},{16,20},{20,16},{24,28},{28,24},{1,5},{5... | collective-permute-start | bytes 393224 | tf_op jit(solution)/shard_map/ppermute | solution.py:448
  29.2 5.7 %collective-permute-start.3 = (bf16[4,128,128]{2,1,0:T(8,128)(2,1)S(1)}, bf16[4,128,128]{2,1,0:T(8,128)(2,1)S(1)}, u32[]{:S(2)}, u32[]{:S(2)}) collective-permute-start(bf16[4,128,128]{2,1,0:T(8,128)(2,1)S(1)} %collective-permute-done.1.refs_5_), channel_id=1, source_target_pairs={{0,4},{4,0},{8,12},{12,8},{16,20},{20,16},{24,28},{28,24},{1,5},{5... | collective-permute-start | bytes 393224 | tf_op jit(solution)/shard_map/ppermute | solution.py:448
  33.4 5.2 %copy-start = (f32[1024]{0:T(1024)S(1)}, f32[1024]{0:T(1024)}, u32[]{:S(2)}) copy-start(f32[1024]{0:T(1024)} %param.13) | copy-start | bytes 12292
  33.4 5.2 %collective-permute-start.5 = (bf16[4,128,128]{2,1,0:T(8,128)(2,1)S(1)}, bf16[4,128,128]{2,1,0:T(8,128)(2,1)S(1)}, u32[]{:S(2)}, u32[]{:S(2)}) collective-permute-start(bf16[4,128,128]{2,1,0:T(8,128)(2,1)S(1)} %collective-permute-done.4.refs_0_.refs_7_), channel_id=1, source_target_pairs={{0,4},{4,0},{8,12},{12,8},{16,20},{20,16},{24,28},{28,24},{1,5},{5... | collective-permute-start | bytes 393224 | tf_op jit(solution)/shard_map/ppermute | solution.py:448
  39.6 1.6 %collective-permute-start.6 = (bf16[128,1024]{1,0:T(8,128)(2,1)S(1)}, bf16[128,1024]{1,0:T(8,128)(2,1)S(1)}, u32[]{:S(2)}, u32[]{:S(2)}) collective-permute-start(bf16[128,1024]{1,0:T(8,128)(2,1)S(1)} %project.7.after), channel_id=1, source_target_pairs={{0,1},{1,0},{2,3},{3,2},{4,5},{5,4},{6,7},{7,6},{8,9},{9,8},{10,11... | collective-permute-start | bytes 786440 | tf_op jit(solution)/shard_map/ppermute | solution.py:484
  41.7 9.5 %collective-permute-start.9 = (bf16[128,1024]{1,0:T(8,128)(2,1)S(1)}, bf16[128,1024]{1,0:T(8,128)(2,1)S(1)}, u32[]{:S(2)}, u32[]{:S(2)}) collective-permute-start(bf16[128,1024]{1,0:T(8,128)(2,1)S(1)} %project.8.after), channel_id=1, source_target_pairs={{0,2},{1,3},{2,0},{3,1},{4,6},{5,7},{6,4},{7,5},{8,10},{9,11},{10,... | collective-permute-start | bytes 786440 | tf_op jit(solution)/shard_map/ppermute | solution.py:493
  44.2 2.4 %collective-permute-start.7 = (bf16[384,1024]{1,0:T(8,128)(2,1)S(1)}, bf16[384,1024]{1,0:T(8,128)(2,1)S(1)}, u32[]{:S(2)}, u32[]{:S(2)}) collective-permute-start(bf16[384,1024]{1,0:T(8,128)(2,1)S(1)} %project.9.after), channel_id=1, source_target_pairs={{0,1},{1,0},{2,3},{3,2},{4,5},{5,4},{6,7},{7,6},{8,9},{9,8},{10,11... | collective-permute-start | bytes 2359304 | tf_op jit(solution)/shard_map/ppermute | solution.py:484
  45.6 5.6 %collective-permute-start.8 = (bf16[512,1024]{1,0:T(8,128)(2,1)S(1)}, bf16[512,1024]{1,0:T(8,128)(2,1)S(1)}, u32[]{:S(2)}, u32[]{:S(2)}) collective-permute-start(bf16[512,1024]{1,0:T(8,128)(2,1)S(1)} %project.10.after), channel_id=1, source_target_pairs={{0,1},{1,0},{2,3},{3,2},{4,5},{5,4},{6,7},{7,6},{8,9},{9,8},{10,11... | collective-permute-start | bytes 3145736 | tf_op jit(solution)/shard_map/ppermute | solution.py:503
  47.3 14.8 %collective-permute-start.10 = (bf16[256,1024]{1,0:T(8,128)(2,1)S(1)}, bf16[256,1024]{1,0:T(8,128)(2,1)S(1)}, u32[]{:S(2)}, u32[]{:S(2)}) collective-permute-start(bf16[256,1024]{1,0:T(8,128)(2,1)S(1)} %project.11.after), channel_id=1, source_target_pairs={{0,2},{1,3},{2,0},{3,1},{4,6},{5,7},{6,4},{7,5},{8,10},{9,11},{10,... | collective-permute-start | bytes 1572872 | tf_op jit(solution)/shard_map/ppermute | solution.py:493
  48.4 18.6 %collective-permute-start.11 = (bf16[128,1024]{1,0:T(8,128)(2,1)S(1)}, bf16[128,1024]{1,0:T(8,128)(2,1)S(1)}, u32[]{:S(2)}, u32[]{:S(2)}) collective-permute-start(bf16[128,1024]{1,0:T(8,128)(2,1)S(1)} %project.12.after), channel_id=1, source_target_pairs={{0,2},{1,3},{2,0},{3,1},{4,6},{5,7},{6,4},{7,5},{8,10},{9,11},{10,... | collective-permute-start | bytes 786440 | tf_op jit(solution)/shard_map/ppermute | solution.py:493

commit v3 on v2

--- a/solution.py
+++ b/solution.py
@@ -42,7 +42,7 @@
 
 
 def keys_values_body(
-    width, x_hbm, wk_hbm, wv_hbm, wq_hbm, x, wq, k_ref, vt_ref, keep_ref, give_ref, wk, wv, k_acc, v_acc, s, sem
+    width, x_hbm, wk_hbm, wv_hbm, wq_hbm, x, wq, k_ref, vt_ref, keep_ref, give_ref, wk, wv, k_acc, v_acc, s, vt, sem, vt_sem
 ):
     rows, depth = x.shape
     size = wk.shape[1]
@@ -70,18 +70,21 @@
         term = mm(x[:, a], wk[a, :])
         k_acc[...] = term if c == 0 else k_acc[...] + term
         for h in range(c * heads // cuts, (c + 1) * heads // cuts):
-            vt_ref[own[h], :] = v_acc[:, own[h]].T.astype(bf16)
+            vt[own[h], :] = v_acc[:, own[h]].T.astype(bf16)
+    vt_out = pltpu.make_async_copy(vt, vt_ref, vt_sem)
+    vt_out.start()
     for h in range(heads):
         raw = k_acc[:, own[h]]
         key = (raw * lax.rsqrt(jnp.sum(raw * raw, axis=-1, keepdims=True) + eps)).astype(bf16)
         k_ref[:, own[h]] = key
-        s[h] = mm(vt_ref[own[h], :], key).astype(bf16)
+        s[h] = mm(vt[own[h], :], key).astype(bf16)
     first = (lax.axis_index("seq") & 1) * half
     for h in range(half):
         keep_ref[h] = s[first + h]
         give_ref[h] = s[half - first + h]
     for copy in q_in:
         copy.wait()
+    vt_out.wait()
 
 
 def keys_values(tokens, w_key, w_value, w_query, width):
@@ -108,9 +111,11 @@
             pltpu.VMEM((rows, size), f32),
             pltpu.VMEM((rows, size), f32),
             pltpu.VMEM((heads, width, width), bf16),
+            pltpu.VMEM((size, rows), bf16),
             pltpu.SemaphoreType.DMA((4, cuts)),
+            pltpu.SemaphoreType.DMA,
         ],
-        compiler_params=params(30),
+        compiler_params=params(34),
         cost_estimate=cost(4 * rows * depth * size, 2 * (rows * depth + 2 * depth * size)),
         name="keys_values",
     )(in_hbm(tokens), in_hbm(w_key), in_hbm(w_value), in_hbm(w_query))
@@ -199,14 +204,15 @@
         meanwhile(c, cuts)
 
 
-def queries_first_body(x, wq, lam_hbm, prior_hbm, after, raw_ref, lam, prior, sem):
+def queries_first_body(x, wq, lam_hbm, prior_hbm, after, raw_ref, lam, prior, acc, sem):
     copies = [pltpu.make_async_copy(lam_hbm, lam, sem.at[0])]
     heads = prior.shape[1]
     for p in range(prior.shape[0]):
         for h in range(heads):
             copies.append(pltpu.make_async_copy(prior_hbm.at[p, h], prior.at[p, h], sem.at[1 + p * heads + h]))
     starts(copies)
-    query_product(x, wq, raw_ref, 0, lambda c, cuts: None)
+    query_product(x, wq, acc, 0, lambda c, cuts: None)
+    raw_ref[...] = acc[...]
     for copy in copies:
         copy.wait()
 
@@ -224,14 +230,14 @@
             pltpu.VMEM(level_weights.shape, f32),
             pltpu.VMEM(prior_states.shape, f32),
         ],
-        scratch_shapes=[pltpu.SemaphoreType.DMA((1 + priors * heads,))],
+        scratch_shapes=[pltpu.VMEM((rows, size), f32), pltpu.SemaphoreType.DMA((1 + priors * heads,))],
         compiler_params=params(16),
         cost_estimate=cost(2 * rows * depth * size, 2 * (rows * depth + depth * size)),
         name="queries_first",
     )(tokens, w_query, in_hbm(level_weights), in_hbm(prior_states), after)
 
 
-def queries_second_body(width, x, wq, raw_old, w_hbm, after, qt_ref, raw_ref, w_ref, sem):
+def queries_second_body(width, x, wq, raw_old, w_hbm, after, qt_ref, raw_ref, w_ref, qt, acc, sem):
     copies = row_copies(w_hbm, 0, w_ref, sem, 0, sem.shape[0])
     starts(copies)
     heads = raw_old.shape[1] // width
@@ -239,9 +245,11 @@
     def meanwhile(c, cuts):
         for h in range(c * heads // cuts, (c + 1) * heads // cuts):
             own = slice(h * width, (h + 1) * width)
-            leave_tiles(qt_ref, own, finished(raw_old[:, own]))
-
-    query_product(x, wq, raw_ref, raw_old.shape[1], meanwhile)
+            leave_tiles(qt, own, finished(raw_old[:, own]))
+
+    query_product(x, wq, acc, raw_old.shape[1], meanwhile)
+    raw_ref[...] = acc[...]
+    qt_ref[...] = qt[...]
     for copy in copies:
         copy.wait()
 
@@ -258,7 +266,11 @@
             pltpu.VMEM((rows, size), f32),
             pltpu.VMEM((w_out.shape[0] // 2, w_out.shape[1]), bf16),
         ],
-        scratch_shapes=[pltpu.SemaphoreType.DMA((w_out.shape[0] // 32,))],
+        scratch_shapes=[
+            pltpu.VMEM((rows // TILE, size, TILE), bf16),
+            pltpu.VMEM((rows, size), f32),
+            pltpu.SemaphoreType.DMA((w_out.shape[0] // 32,)),
+        ],
         compiler_params=params(16),
         cost_estimate=cost(2 * rows * depth * size, 2 * (rows * depth + depth * size)),
         name="queries_second",
@@ -497,7 +509,14 @@
     ahead = far_part(acc, queries_t, acc, states, level_weights, gain, width, 0, 1)
     after, ahead_gots = shared(ahead, ahead)
     rest = far_part(after, queries_t, acc, states, level_weights, gain, width, 1, rows // TILE - 1)
-    after = onward(rest, ahead, ahead_gots, 0, TILE)
+    after = rest
+    terms = []
+    for d in range(1, chips):
+        after = project(after, weights, 0, d, groups, [ahead], f32)
+        total = (after + ahead_gots[d - 1].astype(f32)).astype(bf16)
+        terms.append(lax.ppermute(total, "head", [(i, (i + 2 * d) % groups) for i in range(groups)]))
+    received.append(terms)
+    after = total
     after, rest_gots = shared(after, rest)
     after = project(after, weights, 1, 0, groups, [ahead, rest], bf16, estimate=FAR_APART)
     other = lax.ppermute(after, "head", twin)

time: 67.9 us -> 67.9 us (level)
    ppermute x0 -> x1, starting transfers between devices: none -> 1.55 us  [per_device(): lax.ppermute(total, 'head', [(i, (i + 2 * d) % groups) for i in range(gro...]
    ppermute x3 -> x2, starting transfers between devices: 3.69 us -> 2.16 us  [onward(): lax.ppermute(after, 'head', [(i, (i + 2 * d) % groups) for i in range(gro...]
    pallas_call x1, Pallas kernels: 11.9 us -> 12.6 us  [keys_values(): pl.pallas_call(functools.partial(keys_values_body, width), in_specs=[HBM]...]
    ppermute x3 -> x2, waiting for transfers between devices: 14 us -> 14.3 us  [onward(): lax.ppermute(after, 'head', [(i, (i + 2 * d) % groups) for i in range(gro...]
where the time goes in v3:
time: 67.9 us; the launch traced here: 67.7 us
  Pallas kernels  35.1 us (52%)
  waiting for transfers between devices  17.5 us (26%)
  starting transfers between devices  14.7 us (22%)
    ppermute x2, waiting for transfers between devices, onward(): lax.ppermute(after, 'head', [(i, (i + 2 * d) % groups) for i in range(gro...  14.3 us
    pallas_call x1, Pallas kernels, keys_values(): pl.pallas_call(functools.partial(keys_values_body, width), in_specs=[HBM]...  12.6 us
    ppermute x6, starting transfers between devices, send(): return lax.ppermute(state, 'seq', [(r, r ^ 1 << j) for r in range(count)])  10.3 us
    pallas_call x7, Pallas kernels, project(): pl.pallas_call(functools.partial(project_body, flip, d, groups, start, ta...  5.65 us
    pallas_call x1, Pallas kernels, queries_second(): pl.pallas_call(functools.partial(queries_second_body, width), in_specs=[V...  4.14 us
    pallas_call x1, Pallas kernels, queries_first(): pl.pallas_call(queries_first_body, in_specs=[VMEM, VMEM, HBM, HBM, ANY],...  3.68 us
    ppermute x6, waiting for transfers between devices, send(): return lax.ppermute(state, 'seq', [(r, r ^ 1 << j) for r in range(count)])  2.63 us
    pallas_call x1, Pallas kernels, attention(): pl.pallas_call(functools.partial(attention_body, width), in_specs=[VMEM]...  2.58 us
  transfers between devices with their start and end apart: 12, of which 7 were waited for; matrix products, arithmetic and copies ran while one was open for 0% of the time, Pallas kernels for 31%

profile of v3, /device:TPU:0, one launch (start us, length us, event | category | flops | bytes accessed | tf_op | source)
XLA Modules:
  0.0 67.7 jit_solution(2844210678448465109)
XLA Ops:
  0.0 12.6 %keys_values.1 = (bf16[512,4096]{1,0:T(8,128)(2,1)S(1)}, bf16[4096,1024]{1,0:T(8,128)(2,1)S(1)}, bf16[512,1024]{1,0:T(8,128)(2,1)S(1)}, bf16[1024,512]{1,0:T(8,1...) custom-call(bf16[512,4096]{1,0:T(8,128)(2,1)} %x_hbm.1, bf16[4096,1024]{1,0:T(8,128)(2,1)} %wk_hbm.1, ...), custom_call_target="tpu_custom_call" | custom-call | flops 85899344 | bytes 209715 | tf_op jit(solution)/shard_map/keys_values/pallas_call | solution.py:96
  12.6 3.0 %collective-permute-start = (bf16[4,128,128]{2,1,0:T(8,128)(2,1)S(1)}, bf16[4,128,128]{2,1,0:T(8,128)(2,1)S(1)}, u32[]{:S(2)}, u32[]{:S(2)}) collective-permute-start(bf16[4,128,128]{2,1,0:T(8,128)(2,1)S(1)} %get-tuple-element.30), channel_id=1, source_target_pairs={{0,4},{4,0},{8,12},{12,8},{16,20},{20,16},{24,28},{28,24},{1,5},{5... | collective-permute-start | bytes 393224 | tf_op jit(solution)/shard_map/ppermute | solution.py:460
  15.7 3.7 %queries_first.1 = (f32[512,512]{1,0:T(8,128)S(1)}, f32[21,8,512]{2,1,0:T(8,128)S(1)}, f32[4,8,128,128]{3,2,1,0:T(8,128)S(1)}) custom-call(bf16[512,4096]{1,0:T(8,128)(2,1)S(1)} %get-tuple-element.25.x, bf16[4096,1024]{1,0:T(8,128)(2,1)S(1)} %get-tuple-element.26.wq, f32[21,8,512]{2,1,0:T(8,128)} %lam_hbm.1, f32[4,8,128,128]{3,2,1,0:T(8,128)} %prior_hbm.1, ...), custom_call_target="tpu_custom_call" | custom-call | flops 21474836 | bytes 83886 | tf_op jit(solution)/shard_map/queries_first/pallas_call | solution.py:224
  19.4 1.7 %collective-permute-start.1 = (bf16[4,128,128]{2,1,0:T(8,128)(2,1)S(1)}, bf16[4,128,128]{2,1,0:T(8,128)(2,1)S(1)}, u32[]{:S(2)}, u32[]{:S(2)}) collective-permute-start(bf16[4,128,128]{2,1,0:T(8,128)(2,1)S(1)} %add_convert_fusion.2.after), channel_id=1, source_target_pairs={{0,8},{4,12},{8,0},{12,4},{16,24},{20,28},{24,16},{28,20},{1,9},{5... | collective-permute-start | bytes 393224 | tf_op jit(solution)/shard_map/ppermute | solution.py:460
  21.1 4.1 %queries_second.1 = (bf16[4,512,128]{2,1,0:T(8,128)(2,1)S(1)}, f32[512,512]{1,0:T(8,128)S(1)}, bf16[512,4096]{1,0:T(8,128)(2,1)S(1)}) custom-call(bf16[512,4096]{1,0:T(8,128)(2,1)S(1)} %get-tuple-element.25.x, bf16[4096,1024]{1,0:T(8,128)(2,1)S(1)} %get-tuple-element.26.wq, f32[512,512]{1,0:T(8,128)S(1)} %get-tuple-element.31.raw_old, ...), custom_call_target="tpu_custom_call" | custom-call | flops 21474836 | bytes 83886 | tf_op jit(solution)/shard_map/queries_second/pallas_call | solution.py:260
  25.3 2.7 %collective-permute-start.4 = (bf16[4,128,128]{2,1,0:T(8,128)(2,1)S(1)}, bf16[4,128,128]{2,1,0:T(8,128)(2,1)S(1)}, u32[]{:S(2)}, u32[]{:S(2)}) collective-permute-start(bf16[4,128,128]{2,1,0:T(8,128)(2,1)S(1)} %add_convert_fusion.1.after), channel_id=1, source_target_pairs={{0,16},{4,20},{8,24},{12,28},{16,0},{20,4},{24,8},{28,12},{1,17},{... | collective-permute-start | bytes 393224 | tf_op jit(solution)/shard_map/ppermute | solution.py:460
  27.9 1.5 %collective-permute-start.2 = (bf16[4,128,128]{2,1,0:T(8,128)(2,1)S(1)}, bf16[4,128,128]{2,1,0:T(8,128)(2,1)S(1)}, u32[]{:S(2)}, u32[]{:S(2)}) collective-permute-start(bf16[4,128,128]{2,1,0:T(8,128)(2,1)S(1)} %get-tuple-element.40.after), channel_id=1, source_target_pairs={{0,4},{4,0},{8,12},{12,8},{16,20},{20,16},{24,28},{28,24},{1,5},{5... | collective-permute-start | bytes 393224 | tf_op jit(solution)/shard_map/ppermute | solution.py:460
  30.0 2.6 %attention.1 = (f32[4,1024,128]{2,1,0:T(8,128)S(1)}, bf16[4,512,128]{2,1,0:T(8,128)(2,1)S(1)}) custom-call(f32[21,8,512]{2,1,0:T(8,128)S(1)} %get-tuple-element.28.lam_ref.refs_9_, f32[4,8,128,128]{3,2,1,0:T(8,128)S(1)} %get-tuple-element.29.prior_ref, bf16[4,128,128]{2,1,0:T(8,128)(2,1)S(1)} %add_convert_fusion.1.after, ...), custom_call_target="tpu_custom_call" | custom-call | flops 40000000000 | bytes 100000000 | tf_op jit(solution)/shard_map/attention/pallas_call | solution.py:299
  32.6 1.1 %collective-permute-done.4.refs_0_.refs_7_ = bf16[4,128,128]{2,1,0:T(8,128)(2,1)S(1)} collective-permute-done((bf16[4,128,128]{2,1,0:T(8,128)(2,1)S(1)}, bf16[4,128,128]{2,1,0:T(8,128)(2,1)S(1)}, u32[]{:S(2)}, u32[]{:S(2)}) %collective-permute-start.4) | collective-permute-done | bytes 131104 | tf_op jit(solution)/shard_map/ppermute | solution.py:460
  33.6 0.9 %collective-permute-start.5 = (bf16[4,128,128]{2,1,0:T(8,128)(2,1)S(1)}, bf16[4,128,128]{2,1,0:T(8,128)(2,1)S(1)}, u32[]{:S(2)}, u32[]{:S(2)}) collective-permute-start(bf16[4,128,128]{2,1,0:T(8,128)(2,1)S(1)} %collective-permute-done.4.refs_0_.refs_7_), channel_id=1, source_target_pairs={{0,4},{4,0},{8,12},{12,8},{16,20},{20,16},{24,28},{28,24},{1,5},{5... | collective-permute-start | bytes 393224 | tf_op jit(solution)/shard_map/ppermute | solution.py:460
  35.1 2.5 %fetch.1.w_low = bf16[512,4096]{1,0:T(8,128)(2,1)S(1)} custom-call(bf16[1024,4096]{1,0:T(8,128)(2,1)} %w_hbm.3, bf16[4,128,128]{2,1,0:T(8,128)(2,1)S(1)} %collective-permute-done.4.refs_0_.refs_7_, bf16[4,128,128]{2,1,0:T(8,128)(2,1)S(1)} %collective-permute-done.2.refs_1_.refs_4_, bf16[4,128,128]{2,1,0:T(8,128)(2,1)S(1)} %collective-permute-done.3.refs_2_.refs_6_), custom_call_target="tpu_custom_call" | custom-call | bytes 83886 | tf_op jit(solution)/shard_map/fetch/pallas_call | solution.py:320
  37.6 1.0 %collective-permute-done.5.refs_8_ = bf16[4,128,128]{2,1,0:T(8,128)(2,1)S(1)} collective-permute-done((bf16[4,128,128]{2,1,0:T(8,128)(2,1)S(1)}, bf16[4,128,128]{2,1,0:T(8,128)(2,1)S(1)}, u32[]{:S(2)}, u32[]{:S(2)}) %collective-permute-start.5) | collective-permute-done | bytes 131104 | tf_op jit(solution)/shard_map/ppermute | solution.py:460
  39.7 1.0 %far_part.3.after.refs_0_.refs_1_ = bf16[384,1024]{1,0:T(8,128)(2,1)S(1)} custom-call(bf16[128,1024]{1,0:T(8,128)(2,1)S(1)} %project.7.after, bf16[4,512,128]{2,1,0:T(8,128)(2,1)S(1)} %get-tuple-element.35.qt_old.refs_0_, bf16[4,512,128]{2,1,0:T(8,128)(2,1)S(1)} %get-tuple-element.39.refs_1_, f32[4,1024,128]{2,1,0:T(8,128)S(1)} %get-tuple-element.38.after.refs_2_, ...), custom_call_target="tpu_custom_call" | custom-call | flops 5368709 | bytes 41943 | tf_op jit(solution)/shard_map/far_part/pallas_call | solution.py:378
  41.3 1.6 %collective-permute-start.9 = (bf16[128,1024]{1,0:T(8,128)(2,1)S(1)}, bf16[128,1024]{1,0:T(8,128)(2,1)S(1)}, u32[]{:S(2)}, u32[]{:S(2)}) collective-permute-start(bf16[128,1024]{1,0:T(8,128)(2,1)S(1)} %add_convert_fusion.after), channel_id=1, source_target_pairs={{0,2},{1,3},{2,0},{3,1},{4,6},{5,7},{6,4},{7,5},{8,10},{9,11},{10,... | collective-permute-start | bytes 786440 | tf_op jit(solution)/shard_map/ppermute | solution.py:517
  42.9 1.0 %project.9.after = bf16[384,1024]{1,0:T(8,128)(2,1)S(1)} custom-call(bf16[128,1024]{1,0:T(8,128)(2,1)S(1)} %add_convert_fusion.after, bf16[512,4096]{1,0:T(8,128)(2,1)S(1)} %get-tuple-element.44.w_top, bf16[512,4096]{1,0:T(8,128)(2,1)S(1)} %fetch.1.w_low, bf16[384,1024]{1,0:T(8,128)(2,1)S(1)} %far_part.3.after.refs_0_.refs_1_), custom_call_target="tpu_custom_call" | custom-call | flops 8053063 | bytes 20971 | tf_op jit(solution)/shard_map/project/pallas_call | solution.py:413
  44.1 1.3 %project.10.after = bf16[512,1024]{1,0:T(8,128)(2,1)S(1)} custom-call(bf16[384,1024]{1,0:T(8,128)(2,1)S(1)} %project.9.after, bf16[512,4096]{1,0:T(8,128)(2,1)S(1)} %get-tuple-element.44.w_top, bf16[512,4096]{1,0:T(8,128)(2,1)S(1)} %fetch.1.w_low, bf16[128,1024]{1,0:T(8,128)(2,1)S(1)} %far_part.2.after.refs_0_, ...), custom_call_target="tpu_custom_call" | custom-call | flops 40000000000 | bytes 100000000 | tf_op jit(solution)/shard_map/project/pallas_call | solution.py:413
  46.2 0.7 %project.11.after = bf16[256,1024]{1,0:T(8,128)(2,1)S(1)} custom-call(bf16[512,1024]{1,0:T(8,128)(2,1)S(1)} %project.10.after, bf16[512,4096]{1,0:T(8,128)(2,1)S(1)} %get-tuple-element.44.w_top, bf16[512,4096]{1,0:T(8,128)(2,1)S(1)} %fetch.1.w_low, bf16[384,1024]{1,0:T(8,128)(2,1)S(1)} %far_part.3.after.refs_0_.refs_1_, ...), custom_call_target="tpu_custom_call" | custom-call | flops 40000000000 | bytes 100000000 | tf_op jit(solution)/shard_map/project/pallas_call | solution.py:413
  48.0 1.6 %collective-permute-start.11 = (bf16[128,1024]{1,0:T(8,128)(2,1)S(1)}, bf16[128,1024]{1,0:T(8,128)(2,1)S(1)}, u32[]{:S(2)}, u32[]{:S(2)}) collective-permute-start(bf16[128,1024]{1,0:T(8,128)(2,1)S(1)} %project.12.after), channel_id=1, source_target_pairs={{0,2},{1,3},{2,0},{3,1},{4,6},{5,7},{6,4},{7,5},{8,10},{9,11},{10,... | collective-permute-start | bytes 786440 | tf_op jit(solution)/shard_map/ppermute | solution.py:505
  49.6 1.3 %project.13.own_ref = f32[512,1024]{1,0:T(8,128)S(1)} custom-call(bf16[128,1024]{1,0:T(8,128)(2,1)S(1)} %project.12.after, bf16[512,4096]{1,0:T(8,128)(2,1)S(1)} %get-tuple-element.44.w_top, bf16[512,4096]{1,0:T(8,128)(2,1)S(1)} %fetch.1.w_low, bf16[128,1024]{1,0:T(8,128)(2,1)S(1)} %far_part.2.after.refs_0_, bf16[384,1024]{1,0:T(8,128)(2,1)S(1)} %far_part.3.after.refs_0_.refs_1_), custom_call_target="tpu_custom_call" | custom-call | flops 10737418 | bytes 20971 | tf_op jit(solution)/shard_map/project/pallas_call | solution.py:413
  50.9 0.8 %finish.3.out_in = bf16[512,1024]{1,0:T(8,128)(2,1)} custom-call(f32[1,1024]{1,0:T(1,128)S(1)} %bitcast.3, f32[512,1024]{1,0:T(8,128)S(1)} %project.13.own_ref, bf16[512,1024]{1,0:T(8,128)(2,1)S(1)} %collective-permute-done.8.refs_0_, bf16[128,1024]{1,0:T(8,128)(2,1)S(1)} %collective-permute-done.9.refs_1_), custom_call_target="tpu_custom_call" | custom-call | flops 40000000000 | bytes 100000000 | tf_op jit(solution)/shard_map/finish/pallas_call | solution.py:435
  51.7 10.1 %collective-permute-done.10.refs_1_ = bf16[256,1024]{1,0:T(8,128)(2,1)S(1)} collective-permute-done((bf16[256,1024]{1,0:T(8,128)(2,1)S(1)}, bf16[256,1024]{1,0:T(8,128)(2,1)S(1)}, u32[]{:S(2)}, u32[]{:S(2)}) %collective-permute-start.10) | collective-permute-done | bytes 524320 | tf_op jit(solution)/shard_map/ppermute | solution.py:505
  61.8 0.9 %finish.4.out_in = bf16[512,1024]{1,0:T(8,128)(2,1)} custom-call(bf16[512,1024]{1,0:T(8,128)(2,1)} %finish.3.out_in, f32[512,1024]{1,0:T(8,128)S(1)} %project.13.own_ref, bf16[512,1024]{1,0:T(8,128)(2,1)S(1)} %collective-permute-done.8.refs_0_, bf16[256,1024]{1,0:T(8,128)(2,1)S(1)} %collective-permute-done.10.refs_1_), custom_call_target="tpu_custom_call", output_to_operand_aliasing={{}: (0, {})} | custom-call | flops 40000000000 | bytes 100000000 | tf_op jit(solution)/shard_map/finish/pallas_call | solution.py:435
  62.7 4.2 %collective-permute-done.11.refs_1_ = bf16[128,1024]{1,0:T(8,128)(2,1)S(1)} collective-permute-done((bf16[128,1024]{1,0:T(8,128)(2,1)S(1)}, bf16[128,1024]{1,0:T(8,128)(2,1)S(1)}, u32[]{:S(2)}, u32[]{:S(2)}) %collective-permute-start.11) | collective-permute-done | bytes 262176 | tf_op jit(solution)/shard_map/ppermute | solution.py:505
  66.9 0.8 %finish.5 = bf16[512,1024]{1,0:T(8,128)(2,1)} custom-call(bf16[512,1024]{1,0:T(8,128)(2,1)} %finish.4.out_in, f32[512,1024]{1,0:T(8,128)S(1)} %project.13.own_ref, bf16[512,1024]{1,0:T(8,128)(2,1)S(1)} %collective-permute-done.8.refs_0_, bf16[128,1024]{1,0:T(8,128)(2,1)S(1)} %collective-permute-done.11.refs_1_), custom_call_target="tpu_custom_call", output_to_operand_aliasing={{}: (0, {})} | custom-call | flops 40000000000 | bytes 100000000 | tf_op jit(solution)/shard_map/finish/pallas_call | solution.py:435
  (22 shorter events, 4.9 us)
Async XLA Ops:
  12.6 6.7 %collective-permute-start = (bf16[4,128,128]{2,1,0:T(8,128)(2,1)S(1)}, bf16[4,128,128]{2,1,0:T(8,128)(2,1)S(1)}, u32[]{:S(2)}, u32[]{:S(2)}) collective-permute-start(bf16[4,128,128]{2,1,0:T(8,128)(2,1)S(1)} %get-tuple-element.30), channel_id=1, source_target_pairs={{0,4},{4,0},{8,12},{12,8},{16,20},{20,16},{24,28},{28,24},{1,5},{5... | collective-permute-start | bytes 393224 | tf_op jit(solution)/shard_map/ppermute | solution.py:460
  19.4 5.8 %collective-permute-start.1 = (bf16[4,128,128]{2,1,0:T(8,128)(2,1)S(1)}, bf16[4,128,128]{2,1,0:T(8,128)(2,1)S(1)}, u32[]{:S(2)}, u32[]{:S(2)}) collective-permute-start(bf16[4,128,128]{2,1,0:T(8,128)(2,1)S(1)} %add_convert_fusion.2.after), channel_id=1, source_target_pairs={{0,8},{4,12},{8,0},{12,4},{16,24},{20,28},{24,16},{28,20},{1,9},{5... | collective-permute-start | bytes 393224 | tf_op jit(solution)/shard_map/ppermute | solution.py:460
  25.3 8.3 %collective-permute-start.4 = (bf16[4,128,128]{2,1,0:T(8,128)(2,1)S(1)}, bf16[4,128,128]{2,1,0:T(8,128)(2,1)S(1)}, u32[]{:S(2)}, u32[]{:S(2)}) collective-permute-start(bf16[4,128,128]{2,1,0:T(8,128)(2,1)S(1)} %add_convert_fusion.1.after), channel_id=1, source_target_pairs={{0,16},{4,20},{8,24},{12,28},{16,0},{20,4},{24,8},{28,12},{1,17},{... | collective-permute-start | bytes 393224 | tf_op jit(solution)/shard_map/ppermute | solution.py:460
  27.9 6.6 %collective-permute-start.2 = (bf16[4,128,128]{2,1,0:T(8,128)(2,1)S(1)}, bf16[4,128,128]{2,1,0:T(8,128)(2,1)S(1)}, u32[]{:S(2)}, u32[]{:S(2)}) collective-permute-start(bf16[4,128,128]{2,1,0:T(8,128)(2,1)S(1)} %get-tuple-element.40.after), channel_id=1, source_target_pairs={{0,4},{4,0},{8,12},{12,8},{16,20},{20,16},{24,28},{28,24},{1,5},{5... | collective-permute-start | bytes 393224 | tf_op jit(solution)/shard_map/ppermute | solution.py:460
  29.5 5.7 %collective-permute-start.3 = (bf16[4,128,128]{2,1,0:T(8,128)(2,1)S(1)}, bf16[4,128,128]{2,1,0:T(8,128)(2,1)S(1)}, u32[]{:S(2)}, u32[]{:S(2)}) collective-permute-start(bf16[4,128,128]{2,1,0:T(8,128)(2,1)S(1)} %collective-permute-done.1.refs_5_), channel_id=1, source_target_pairs={{0,4},{4,0},{8,12},{12,8},{16,20},{20,16},{24,28},{28,24},{1,5},{5... | collective-permute-start | bytes 393224 | tf_op jit(solution)/shard_map/ppermute | solution.py:460
  33.6 5.0 %copy-start = (f32[1024]{0:T(1024)S(1)}, f32[1024]{0:T(1024)}, u32[]{:S(2)}) copy-start(f32[1024]{0:T(1024)} %param.13) | copy-start | bytes 12292
  33.6 5.0 %collective-permute-start.5 = (bf16[4,128,128]{2,1,0:T(8,128)(2,1)S(1)}, bf16[4,128,128]{2,1,0:T(8,128)(2,1)S(1)}, u32[]{:S(2)}, u32[]{:S(2)}) collective-permute-start(bf16[4,128,128]{2,1,0:T(8,128)(2,1)S(1)} %collective-permute-done.4.refs_0_.refs_7_), channel_id=1, source_target_pairs={{0,4},{4,0},{8,12},{12,8},{16,20},{20,16},{24,28},{28,24},{1,5},{5... | collective-permute-start | bytes 393224 | tf_op jit(solution)/shard_map/ppermute | solution.py:460
  39.6 1.6 %collective-permute-start.6 = (bf16[128,1024]{1,0:T(8,128)(2,1)S(1)}, bf16[128,1024]{1,0:T(8,128)(2,1)S(1)}, u32[]{:S(2)}, u32[]{:S(2)}) collective-permute-start(bf16[128,1024]{1,0:T(8,128)(2,1)S(1)} %project.7.after), channel_id=1, source_target_pairs={{0,1},{1,0},{2,3},{3,2},{4,5},{5,4},{6,7},{7,6},{8,9},{9,8},{10,11... | collective-permute-start | bytes 786440 | tf_op jit(solution)/shard_map/ppermute | solution.py:496
  41.3 9.5 %collective-permute-start.9 = (bf16[128,1024]{1,0:T(8,128)(2,1)S(1)}, bf16[128,1024]{1,0:T(8,128)(2,1)S(1)}, u32[]{:S(2)}, u32[]{:S(2)}) collective-permute-start(bf16[128,1024]{1,0:T(8,128)(2,1)S(1)} %add_convert_fusion.after), channel_id=1, source_target_pairs={{0,2},{1,3},{2,0},{3,1},{4,6},{5,7},{6,4},{7,5},{8,10},{9,11},{10,... | collective-permute-start | bytes 786440 | tf_op jit(solution)/shard_map/ppermute | solution.py:517
  43.9 2.4 %collective-permute-start.7 = (bf16[384,1024]{1,0:T(8,128)(2,1)S(1)}, bf16[384,1024]{1,0:T(8,128)(2,1)S(1)}, u32[]{:S(2)}, u32[]{:S(2)}) collective-permute-start(bf16[384,1024]{1,0:T(8,128)(2,1)S(1)} %project.9.after), channel_id=1, source_target_pairs={{0,1},{1,0},{2,3},{3,2},{4,5},{5,4},{6,7},{7,6},{8,9},{9,8},{10,11... | collective-permute-start | bytes 2359304 | tf_op jit(solution)/shard_map/ppermute | solution.py:496
  45.4 5.5 %collective-permute-start.8 = (bf16[512,1024]{1,0:T(8,128)(2,1)S(1)}, bf16[512,1024]{1,0:T(8,128)(2,1)S(1)}, u32[]{:S(2)}, u32[]{:S(2)}) collective-permute-start(bf16[512,1024]{1,0:T(8,128)(2,1)S(1)} %project.10.after), channel_id=1, source_target_pairs={{0,1},{1,0},{2,3},{3,2},{4,5},{5,4},{6,7},{7,6},{8,9},{9,8},{10,11... | collective-permute-start | bytes 3145736 | tf_op jit(solution)/shard_map/ppermute | solution.py:522
  46.9 14.8 %collective-permute-start.10 = (bf16[256,1024]{1,0:T(8,128)(2,1)S(1)}, bf16[256,1024]{1,0:T(8,128)(2,1)S(1)}, u32[]{:S(2)}, u32[]{:S(2)}) collective-permute-start(bf16[256,1024]{1,0:T(8,128)(2,1)S(1)} %project.11.after), channel_id=1, source_target_pairs={{0,2},{1,3},{2,0},{3,1},{4,6},{5,7},{6,4},{7,5},{8,10},{9,11},{10,... | collective-permute-start | bytes 1572872 | tf_op jit(solution)/shard_map/ppermute | solution.py:505
  48.0 18.9 %collective-permute-start.11 = (bf16[128,1024]{1,0:T(8,128)(2,1)S(1)}, bf16[128,1024]{1,0:T(8,128)(2,1)S(1)}, u32[]{:S(2)}, u32[]{:S(2)}) collective-permute-start(bf16[128,1024]{1,0:T(8,128)(2,1)S(1)} %project.12.after), channel_id=1, source_target_pairs={{0,2},{1,3},{2,0},{3,1},{4,6},{5,7},{6,4},{7,5},{8,10},{9,11},{10,... | collective-permute-start | bytes 786440 | tf_op jit(solution)/shard_map/ppermute | solution.py:505

commit v4 on v3

--- a/solution.py
+++ b/solution.py
@@ -42,7 +42,7 @@
 
 
 def keys_values_body(
-    width, x_hbm, wk_hbm, wv_hbm, wq_hbm, x, wq, k_ref, vt_ref, keep_ref, give_ref, wk, wv, k_acc, v_acc, s, vt, sem, vt_sem
+    width, x_hbm, wk_hbm, wv_hbm, wq_hbm, x, wq, k_ref, vt_ref, keep_ref, give_ref, wk, wv, k_acc, v_acc, s, sem
 ):
     rows, depth = x.shape
     size = wk.shape[1]
@@ -67,24 +67,25 @@
         v_acc[...] = term if c == 0 else v_acc[...] + term
     for c, a in enumerate(at):
         k_in[c].wait()
+        for h in range(c * heads // cuts, (c + 1) * heads // cuts):
+            vt_ref[own[h], :] = v_acc[:, own[h]].T.astype(bf16)
+        if c == cuts - 1:
+            for side in (slice(0, half * width), slice(half * width, size)):
+                k_acc[:, side] += mm(x[:, a], wk[a, side])
+            continue
         term = mm(x[:, a], wk[a, :])
         k_acc[...] = term if c == 0 else k_acc[...] + term
-        for h in range(c * heads // cuts, (c + 1) * heads // cuts):
-            vt[own[h], :] = v_acc[:, own[h]].T.astype(bf16)
-    vt_out = pltpu.make_async_copy(vt, vt_ref, vt_sem)
-    vt_out.start()
     for h in range(heads):
         raw = k_acc[:, own[h]]
         key = (raw * lax.rsqrt(jnp.sum(raw * raw, axis=-1, keepdims=True) + eps)).astype(bf16)
         k_ref[:, own[h]] = key
-        s[h] = mm(vt[own[h], :], key).astype(bf16)
+        s[h] = mm(vt_ref[own[h], :], key).astype(bf16)
     first = (lax.axis_index("seq") & 1) * half
     for h in range(half):
         keep_ref[h] = s[first + h]
         give_ref[h] = s[half - first + h]
     for copy in q_in:
         copy.wait()
-    vt_out.wait()
 
 
 def keys_values(tokens, w_key, w_value, w_query, width):
@@ -111,11 +112,9 @@
             pltpu.VMEM((rows, size), f32),
             pltpu.VMEM((rows, size), f32),
             pltpu.VMEM((heads, width, width), bf16),
-            pltpu.VMEM((size, rows), bf16),
             pltpu.SemaphoreType.DMA((4, cuts)),
-            pltpu.SemaphoreType.DMA,
         ],
-        compiler_params=params(34),
+        compiler_params=params(30),
         cost_estimate=cost(4 * rows * depth * size, 2 * (rows * depth + 2 * depth * size)),
         name="keys_values",
     )(in_hbm(tokens), in_hbm(w_key), in_hbm(w_value), in_hbm(w_query))

time: 67.9 us -> 67.2 us (0.990)
    pallas_call x1, Pallas kernels: 12.6 us -> 11.9 us  [keys_values(): pl.pallas_call(functools.partial(keys_values_body, width), in_specs=[HBM]...]
where the time goes in v4:
time: 67.2 us; the launch traced here: 67 us
  Pallas kernels  34.5 us (51%)
  waiting for transfers between devices  17.4 us (26%)
  starting transfers between devices  14.7 us (22%)
    ppermute x2, waiting for transfers between devices, onward(): lax.ppermute(after, 'head', [(i, (i + 2 * d) % groups) for i in range(gro...  14.3 us
    pallas_call x1, Pallas kernels, keys_values(): pl.pallas_call(functools.partial(keys_values_body, width), in_specs=[HBM]...  11.9 us
    ppermute x6, starting transfers between devices, send(): return lax.ppermute(state, 'seq', [(r, r ^ 1 << j) for r in range(count)])  10.3 us
    pallas_call x7, Pallas kernels, project(): pl.pallas_call(functools.partial(project_body, flip, d, groups, start, ta...  5.66 us
    pallas_call x1, Pallas kernels, queries_second(): pl.pallas_call(functools.partial(queries_second_body, width), in_specs=[V...  4.14 us
    pallas_call x1, Pallas kernels, queries_first(): pl.pallas_call(queries_first_body, in_specs=[VMEM, VMEM, HBM, HBM, ANY],...  3.68 us
    ppermute x6, waiting for transfers between devices, send(): return lax.ppermute(state, 'seq', [(r, r ^ 1 << j) for r in range(count)])  2.63 us
    pallas_call x1, Pallas kernels, attention(): pl.pallas_call(functools.partial(attention_body, width), in_specs=[VMEM]...  2.58 us
  transfers between devices with their start and end apart: 12, of which 7 were waited for; matrix products, arithmetic and copies ran while one was open for 0% of the time, Pallas kernels for 31%

profile of v4, /device:TPU:0, one launch (start us, length us, event | category | flops | bytes accessed | tf_op | source)
XLA Modules:
  0.0 67.0 jit_solution(9176269745149987781)
XLA Ops:
  0.0 11.9 %keys_values.1 = (bf16[512,4096]{1,0:T(8,128)(2,1)S(1)}, bf16[4096,1024]{1,0:T(8,128)(2,1)S(1)}, bf16[512,1024]{1,0:T(8,128)(2,1)S(1)}, bf16[1024,512]{1,0:T(8,1...) custom-call(bf16[512,4096]{1,0:T(8,128)(2,1)} %x_hbm.1, bf16[4096,1024]{1,0:T(8,128)(2,1)} %wk_hbm.1, ...), custom_call_target="tpu_custom_call" | custom-call | flops 85899344 | bytes 209715 | tf_op jit(solution)/shard_map/keys_values/pallas_call | solution.py:97
  12.0 3.0 %collective-permute-start = (bf16[4,128,128]{2,1,0:T(8,128)(2,1)S(1)}, bf16[4,128,128]{2,1,0:T(8,128)(2,1)S(1)}, u32[]{:S(2)}, u32[]{:S(2)}) collective-permute-start(bf16[4,128,128]{2,1,0:T(8,128)(2,1)S(1)} %get-tuple-element.30), channel_id=1, source_target_pairs={{0,4},{4,0},{8,12},{12,8},{16,20},{20,16},{24,28},{28,24},{1,5},{5... | collective-permute-start | bytes 393224 | tf_op jit(solution)/shard_map/ppermute | solution.py:459
  15.0 3.7 %queries_first.1 = (f32[512,512]{1,0:T(8,128)S(1)}, f32[21,8,512]{2,1,0:T(8,128)S(1)}, f32[4,8,128,128]{3,2,1,0:T(8,128)S(1)}) custom-call(bf16[512,4096]{1,0:T(8,128)(2,1)S(1)} %get-tuple-element.25.x, bf16[4096,1024]{1,0:T(8,128)(2,1)S(1)} %get-tuple-element.26.wq, f32[21,8,512]{2,1,0:T(8,128)} %lam_hbm.1, f32[4,8,128,128]{3,2,1,0:T(8,128)} %prior_hbm.1, ...), custom_call_target="tpu_custom_call" | custom-call | flops 21474836 | bytes 83886 | tf_op jit(solution)/shard_map/queries_first/pallas_call | solution.py:223
  18.7 1.7 %collective-permute-start.1 = (bf16[4,128,128]{2,1,0:T(8,128)(2,1)S(1)}, bf16[4,128,128]{2,1,0:T(8,128)(2,1)S(1)}, u32[]{:S(2)}, u32[]{:S(2)}) collective-permute-start(bf16[4,128,128]{2,1,0:T(8,128)(2,1)S(1)} %add_convert_fusion.2.after), channel_id=1, source_target_pairs={{0,8},{4,12},{8,0},{12,4},{16,24},{20,28},{24,16},{28,20},{1,9},{5... | collective-permute-start | bytes 393224 | tf_op jit(solution)/shard_map/ppermute | solution.py:459
  20.4 4.1 %queries_second.1 = (bf16[4,512,128]{2,1,0:T(8,128)(2,1)S(1)}, f32[512,512]{1,0:T(8,128)S(1)}, bf16[512,4096]{1,0:T(8,128)(2,1)S(1)}) custom-call(bf16[512,4096]{1,0:T(8,128)(2,1)S(1)} %get-tuple-element.25.x, bf16[4096,1024]{1,0:T(8,128)(2,1)S(1)} %get-tuple-element.26.wq, f32[512,512]{1,0:T(8,128)S(1)} %get-tuple-element.31.raw_old, ...), custom_call_target="tpu_custom_call" | custom-call | flops 21474836 | bytes 83886 | tf_op jit(solution)/shard_map/queries_second/pallas_call | solution.py:259
  24.6 2.7 %collective-permute-start.4 = (bf16[4,128,128]{2,1,0:T(8,128)(2,1)S(1)}, bf16[4,128,128]{2,1,0:T(8,128)(2,1)S(1)}, u32[]{:S(2)}, u32[]{:S(2)}) collective-permute-start(bf16[4,128,128]{2,1,0:T(8,128)(2,1)S(1)} %add_convert_fusion.1.after), channel_id=1, source_target_pairs={{0,16},{4,20},{8,24},{12,28},{16,0},{20,4},{24,8},{28,12},{1,17},{... | collective-permute-start | bytes 393224 | tf_op jit(solution)/shard_map/ppermute | solution.py:459
  27.3 1.5 %collective-permute-start.2 = (bf16[4,128,128]{2,1,0:T(8,128)(2,1)S(1)}, bf16[4,128,128]{2,1,0:T(8,128)(2,1)S(1)}, u32[]{:S(2)}, u32[]{:S(2)}) collective-permute-start(bf16[4,128,128]{2,1,0:T(8,128)(2,1)S(1)} %get-tuple-element.40.after), channel_id=1, source_target_pairs={{0,4},{4,0},{8,12},{12,8},{16,20},{20,16},{24,28},{28,24},{1,5},{5... | collective-permute-start | bytes 393224 | tf_op jit(solution)/shard_map/ppermute | solution.py:459
  29.3 2.6 %attention.1 = (f32[4,1024,128]{2,1,0:T(8,128)S(1)}, bf16[4,512,128]{2,1,0:T(8,128)(2,1)S(1)}) custom-call(f32[21,8,512]{2,1,0:T(8,128)S(1)} %get-tuple-element.28.lam_ref.refs_9_, f32[4,8,128,128]{3,2,1,0:T(8,128)S(1)} %get-tuple-element.29.prior_ref, bf16[4,128,128]{2,1,0:T(8,128)(2,1)S(1)} %add_convert_fusion.1.after, ...), custom_call_target="tpu_custom_call" | custom-call | flops 40000000000 | bytes 100000000 | tf_op jit(solution)/shard_map/attention/pallas_call | solution.py:298
  31.9 1.0 %collective-permute-done.4.refs_0_.refs_7_ = bf16[4,128,128]{2,1,0:T(8,128)(2,1)S(1)} collective-permute-done((bf16[4,128,128]{2,1,0:T(8,128)(2,1)S(1)}, bf16[4,128,128]{2,1,0:T(8,128)(2,1)S(1)}, u32[]{:S(2)}, u32[]{:S(2)}) %collective-permute-start.4) | collective-permute-done | bytes 131104 | tf_op jit(solution)/shard_map/ppermute | solution.py:459
  32.9 0.9 %collective-permute-start.5 = (bf16[4,128,128]{2,1,0:T(8,128)(2,1)S(1)}, bf16[4,128,128]{2,1,0:T(8,128)(2,1)S(1)}, u32[]{:S(2)}, u32[]{:S(2)}) collective-permute-start(bf16[4,128,128]{2,1,0:T(8,128)(2,1)S(1)} %collective-permute-done.4.refs_0_.refs_7_), channel_id=1, source_target_pairs={{0,4},{4,0},{8,12},{12,8},{16,20},{20,16},{24,28},{28,24},{1,5},{5... | collective-permute-start | bytes 393224 | tf_op jit(solution)/shard_map/ppermute | solution.py:459
  34.4 2.5 %fetch.1.w_low = bf16[512,4096]{1,0:T(8,128)(2,1)S(1)} custom-call(bf16[1024,4096]{1,0:T(8,128)(2,1)} %w_hbm.3, bf16[4,128,128]{2,1,0:T(8,128)(2,1)S(1)} %collective-permute-done.4.refs_0_.refs_7_, bf16[4,128,128]{2,1,0:T(8,128)(2,1)S(1)} %collective-permute-done.2.refs_1_.refs_4_, bf16[4,128,128]{2,1,0:T(8,128)(2,1)S(1)} %collective-permute-done.3.refs_2_.refs_6_), custom_call_target="tpu_custom_call" | custom-call | bytes 83886 | tf_op jit(solution)/shard_map/fetch/pallas_call | solution.py:319
  37.0 1.0 %collective-permute-done.5.refs_8_ = bf16[4,128,128]{2,1,0:T(8,128)(2,1)S(1)} collective-permute-done((bf16[4,128,128]{2,1,0:T(8,128)(2,1)S(1)}, bf16[4,128,128]{2,1,0:T(8,128)(2,1)S(1)}, u32[]{:S(2)}, u32[]{:S(2)}) %collective-permute-start.5) | collective-permute-done | bytes 131104 | tf_op jit(solution)/shard_map/ppermute | solution.py:459
  39.0 1.0 %far_part.3.after.refs_0_.refs_1_ = bf16[384,1024]{1,0:T(8,128)(2,1)S(1)} custom-call(bf16[128,1024]{1,0:T(8,128)(2,1)S(1)} %project.7.after, bf16[4,512,128]{2,1,0:T(8,128)(2,1)S(1)} %get-tuple-element.35.qt_old.refs_0_, bf16[4,512,128]{2,1,0:T(8,128)(2,1)S(1)} %get-tuple-element.39.refs_1_, f32[4,1024,128]{2,1,0:T(8,128)S(1)} %get-tuple-element.38.after.refs_2_, ...), custom_call_target="tpu_custom_call" | custom-call | flops 5368709 | bytes 41943 | tf_op jit(solution)/shard_map/far_part/pallas_call | solution.py:377
  40.6 1.6 %collective-permute-start.9 = (bf16[128,1024]{1,0:T(8,128)(2,1)S(1)}, bf16[128,1024]{1,0:T(8,128)(2,1)S(1)}, u32[]{:S(2)}, u32[]{:S(2)}) collective-permute-start(bf16[128,1024]{1,0:T(8,128)(2,1)S(1)} %add_convert_fusion.after), channel_id=1, source_target_pairs={{0,2},{1,3},{2,0},{3,1},{4,6},{5,7},{6,4},{7,5},{8,10},{9,11},{10,... | collective-permute-start | bytes 786440 | tf_op jit(solution)/shard_map/ppermute | solution.py:516
  42.2 1.0 %project.9.after = bf16[384,1024]{1,0:T(8,128)(2,1)S(1)} custom-call(bf16[128,1024]{1,0:T(8,128)(2,1)S(1)} %add_convert_fusion.after, bf16[512,4096]{1,0:T(8,128)(2,1)S(1)} %get-tuple-element.44.w_top, bf16[512,4096]{1,0:T(8,128)(2,1)S(1)} %fetch.1.w_low, bf16[384,1024]{1,0:T(8,128)(2,1)S(1)} %far_part.3.after.refs_0_.refs_1_), custom_call_target="tpu_custom_call" | custom-call | flops 8053063 | bytes 20971 | tf_op jit(solution)/shard_map/project/pallas_call | solution.py:412
  43.4 1.3 %project.10.after = bf16[512,1024]{1,0:T(8,128)(2,1)S(1)} custom-call(bf16[384,1024]{1,0:T(8,128)(2,1)S(1)} %project.9.after, bf16[512,4096]{1,0:T(8,128)(2,1)S(1)} %get-tuple-element.44.w_top, bf16[512,4096]{1,0:T(8,128)(2,1)S(1)} %fetch.1.w_low, bf16[128,1024]{1,0:T(8,128)(2,1)S(1)} %far_part.2.after.refs_0_, ...), custom_call_target="tpu_custom_call" | custom-call | flops 40000000000 | bytes 100000000 | tf_op jit(solution)/shard_map/project/pallas_call | solution.py:412
  45.5 0.7 %project.11.after = bf16[256,1024]{1,0:T(8,128)(2,1)S(1)} custom-call(bf16[512,1024]{1,0:T(8,128)(2,1)S(1)} %project.10.after, bf16[512,4096]{1,0:T(8,128)(2,1)S(1)} %get-tuple-element.44.w_top, bf16[512,4096]{1,0:T(8,128)(2,1)S(1)} %fetch.1.w_low, bf16[384,1024]{1,0:T(8,128)(2,1)S(1)} %far_part.3.after.refs_0_.refs_1_, ...), custom_call_target="tpu_custom_call" | custom-call | flops 40000000000 | bytes 100000000 | tf_op jit(solution)/shard_map/project/pallas_call | solution.py:412
  47.3 1.6 %collective-permute-start.11 = (bf16[128,1024]{1,0:T(8,128)(2,1)S(1)}, bf16[128,1024]{1,0:T(8,128)(2,1)S(1)}, u32[]{:S(2)}, u32[]{:S(2)}) collective-permute-start(bf16[128,1024]{1,0:T(8,128)(2,1)S(1)} %project.12.after), channel_id=1, source_target_pairs={{0,2},{1,3},{2,0},{3,1},{4,6},{5,7},{6,4},{7,5},{8,10},{9,11},{10,... | collective-permute-start | bytes 786440 | tf_op jit(solution)/shard_map/ppermute | solution.py:504
  48.9 1.3 %project.13.own_ref = f32[512,1024]{1,0:T(8,128)S(1)} custom-call(bf16[128,1024]{1,0:T(8,128)(2,1)S(1)} %project.12.after, bf16[512,4096]{1,0:T(8,128)(2,1)S(1)} %get-tuple-element.44.w_top, bf16[512,4096]{1,0:T(8,128)(2,1)S(1)} %fetch.1.w_low, bf16[128,1024]{1,0:T(8,128)(2,1)S(1)} %far_part.2.after.refs_0_, bf16[384,1024]{1,0:T(8,128)(2,1)S(1)} %far_part.3.after.refs_0_.refs_1_), custom_call_target="tpu_custom_call" | custom-call | flops 10737418 | bytes 20971 | tf_op jit(solution)/shard_map/project/pallas_call | solution.py:412
  50.2 0.8 %finish.3.out_in = bf16[512,1024]{1,0:T(8,128)(2,1)} custom-call(f32[1,1024]{1,0:T(1,128)S(1)} %bitcast.3, f32[512,1024]{1,0:T(8,128)S(1)} %project.13.own_ref, bf16[512,1024]{1,0:T(8,128)(2,1)S(1)} %collective-permute-done.8.refs_0_, bf16[128,1024]{1,0:T(8,128)(2,1)S(1)} %collective-permute-done.9.refs_1_), custom_call_target="tpu_custom_call" | custom-call | flops 40000000000 | bytes 100000000 | tf_op jit(solution)/shard_map/finish/pallas_call | solution.py:434
  51.0 10.1 %collective-permute-done.10.refs_1_ = bf16[256,1024]{1,0:T(8,128)(2,1)S(1)} collective-permute-done((bf16[256,1024]{1,0:T(8,128)(2,1)S(1)}, bf16[256,1024]{1,0:T(8,128)(2,1)S(1)}, u32[]{:S(2)}, u32[]{:S(2)}) %collective-permute-start.10) | collective-permute-done | bytes 524320 | tf_op jit(solution)/shard_map/ppermute | solution.py:504
  61.1 0.9 %finish.4.out_in = bf16[512,1024]{1,0:T(8,128)(2,1)} custom-call(bf16[512,1024]{1,0:T(8,128)(2,1)} %finish.3.out_in, f32[512,1024]{1,0:T(8,128)S(1)} %project.13.own_ref, bf16[512,1024]{1,0:T(8,128)(2,1)S(1)} %collective-permute-done.8.refs_0_, bf16[256,1024]{1,0:T(8,128)(2,1)S(1)} %collective-permute-done.10.refs_1_), custom_call_target="tpu_custom_call", output_to_operand_aliasing={{}: (0, {})} | custom-call | flops 40000000000 | bytes 100000000 | tf_op jit(solution)/shard_map/finish/pallas_call | solution.py:434
  62.0 4.2 %collective-permute-done.11.refs_1_ = bf16[128,1024]{1,0:T(8,128)(2,1)S(1)} collective-permute-done((bf16[128,1024]{1,0:T(8,128)(2,1)S(1)}, bf16[128,1024]{1,0:T(8,128)(2,1)S(1)}, u32[]{:S(2)}, u32[]{:S(2)}) %collective-permute-start.11) | collective-permute-done | bytes 262176 | tf_op jit(solution)/shard_map/ppermute | solution.py:504
  66.2 0.8 %finish.5 = bf16[512,1024]{1,0:T(8,128)(2,1)} custom-call(bf16[512,1024]{1,0:T(8,128)(2,1)} %finish.4.out_in, f32[512,1024]{1,0:T(8,128)S(1)} %project.13.own_ref, bf16[512,1024]{1,0:T(8,128)(2,1)S(1)} %collective-permute-done.8.refs_0_, bf16[128,1024]{1,0:T(8,128)(2,1)S(1)} %collective-permute-done.11.refs_1_), custom_call_target="tpu_custom_call", output_to_operand_aliasing={{}: (0, {})} | custom-call | flops 40000000000 | bytes 100000000 | tf_op jit(solution)/shard_map/finish/pallas_call | solution.py:434
  (22 shorter events, 5.0 us)
Async XLA Ops:
  12.0 6.7 %collective-permute-start = (bf16[4,128,128]{2,1,0:T(8,128)(2,1)S(1)}, bf16[4,128,128]{2,1,0:T(8,128)(2,1)S(1)}, u32[]{:S(2)}, u32[]{:S(2)}) collective-permute-start(bf16[4,128,128]{2,1,0:T(8,128)(2,1)S(1)} %get-tuple-element.30), channel_id=1, source_target_pairs={{0,4},{4,0},{8,12},{12,8},{16,20},{20,16},{24,28},{28,24},{1,5},{5... | collective-permute-start | bytes 393224 | tf_op jit(solution)/shard_map/ppermute | solution.py:459
  18.7 5.8 %collective-permute-start.1 = (bf16[4,128,128]{2,1,0:T(8,128)(2,1)S(1)}, bf16[4,128,128]{2,1,0:T(8,128)(2,1)S(1)}, u32[]{:S(2)}, u32[]{:S(2)}) collective-permute-start(bf16[4,128,128]{2,1,0:T(8,128)(2,1)S(1)} %add_convert_fusion.2.after), channel_id=1, source_target_pairs={{0,8},{4,12},{8,0},{12,4},{16,24},{20,28},{24,16},{28,20},{1,9},{5... | collective-permute-start | bytes 393224 | tf_op jit(solution)/shard_map/ppermute | solution.py:459
  24.6 8.3 %collective-permute-start.4 = (bf16[4,128,128]{2,1,0:T(8,128)(2,1)S(1)}, bf16[4,128,128]{2,1,0:T(8,128)(2,1)S(1)}, u32[]{:S(2)}, u32[]{:S(2)}) collective-permute-start(bf16[4,128,128]{2,1,0:T(8,128)(2,1)S(1)} %add_convert_fusion.1.after), channel_id=1, source_target_pairs={{0,16},{4,20},{8,24},{12,28},{16,0},{20,4},{24,8},{28,12},{1,17},{... | collective-permute-start | bytes 393224 | tf_op jit(solution)/shard_map/ppermute | solution.py:459
  27.3 6.6 %collective-permute-start.2 = (bf16[4,128,128]{2,1,0:T(8,128)(2,1)S(1)}, bf16[4,128,128]{2,1,0:T(8,128)(2,1)S(1)}, u32[]{:S(2)}, u32[]{:S(2)}) collective-permute-start(bf16[4,128,128]{2,1,0:T(8,128)(2,1)S(1)} %get-tuple-element.40.after), channel_id=1, source_target_pairs={{0,4},{4,0},{8,12},{12,8},{16,20},{20,16},{24,28},{28,24},{1,5},{5... | collective-permute-start | bytes 393224 | tf_op jit(solution)/shard_map/ppermute | solution.py:459
  28.8 5.7 %collective-permute-start.3 = (bf16[4,128,128]{2,1,0:T(8,128)(2,1)S(1)}, bf16[4,128,128]{2,1,0:T(8,128)(2,1)S(1)}, u32[]{:S(2)}, u32[]{:S(2)}) collective-permute-start(bf16[4,128,128]{2,1,0:T(8,128)(2,1)S(1)} %collective-permute-done.1.refs_5_), channel_id=1, source_target_pairs={{0,4},{4,0},{8,12},{12,8},{16,20},{20,16},{24,28},{28,24},{1,5},{5... | collective-permute-start | bytes 393224 | tf_op jit(solution)/shard_map/ppermute | solution.py:459
  32.9 5.0 %copy-start = (f32[1024]{0:T(1024)S(1)}, f32[1024]{0:T(1024)}, u32[]{:S(2)}) copy-start(f32[1024]{0:T(1024)} %param.13) | copy-start | bytes 12292
  32.9 5.0 %collective-permute-start.5 = (bf16[4,128,128]{2,1,0:T(8,128)(2,1)S(1)}, bf16[4,128,128]{2,1,0:T(8,128)(2,1)S(1)}, u32[]{:S(2)}, u32[]{:S(2)}) collective-permute-start(bf16[4,128,128]{2,1,0:T(8,128)(2,1)S(1)} %collective-permute-done.4.refs_0_.refs_7_), channel_id=1, source_target_pairs={{0,4},{4,0},{8,12},{12,8},{16,20},{20,16},{24,28},{28,24},{1,5},{5... | collective-permute-start | bytes 393224 | tf_op jit(solution)/shard_map/ppermute | solution.py:459
  38.9 1.6 %collective-permute-start.6 = (bf16[128,1024]{1,0:T(8,128)(2,1)S(1)}, bf16[128,1024]{1,0:T(8,128)(2,1)S(1)}, u32[]{:S(2)}, u32[]{:S(2)}) collective-permute-start(bf16[128,1024]{1,0:T(8,128)(2,1)S(1)} %project.7.after), channel_id=1, source_target_pairs={{0,1},{1,0},{2,3},{3,2},{4,5},{5,4},{6,7},{7,6},{8,9},{9,8},{10,11... | collective-permute-start | bytes 786440 | tf_op jit(solution)/shard_map/ppermute | solution.py:495
  40.6 9.5 %collective-permute-start.9 = (bf16[128,1024]{1,0:T(8,128)(2,1)S(1)}, bf16[128,1024]{1,0:T(8,128)(2,1)S(1)}, u32[]{:S(2)}, u32[]{:S(2)}) collective-permute-start(bf16[128,1024]{1,0:T(8,128)(2,1)S(1)} %add_convert_fusion.after), channel_id=1, source_target_pairs={{0,2},{1,3},{2,0},{3,1},{4,6},{5,7},{6,4},{7,5},{8,10},{9,11},{10,... | collective-permute-start | bytes 786440 | tf_op jit(solution)/shard_map/ppermute | solution.py:516
  43.2 2.4 %collective-permute-start.7 = (bf16[384,1024]{1,0:T(8,128)(2,1)S(1)}, bf16[384,1024]{1,0:T(8,128)(2,1)S(1)}, u32[]{:S(2)}, u32[]{:S(2)}) collective-permute-start(bf16[384,1024]{1,0:T(8,128)(2,1)S(1)} %project.9.after), channel_id=1, source_target_pairs={{0,1},{1,0},{2,3},{3,2},{4,5},{5,4},{6,7},{7,6},{8,9},{9,8},{10,11... | collective-permute-start | bytes 2359304 | tf_op jit(solution)/shard_map/ppermute | solution.py:495
  44.7 5.5 %collective-permute-start.8 = (bf16[512,1024]{1,0:T(8,128)(2,1)S(1)}, bf16[512,1024]{1,0:T(8,128)(2,1)S(1)}, u32[]{:S(2)}, u32[]{:S(2)}) collective-permute-start(bf16[512,1024]{1,0:T(8,128)(2,1)S(1)} %project.10.after), channel_id=1, source_target_pairs={{0,1},{1,0},{2,3},{3,2},{4,5},{5,4},{6,7},{7,6},{8,9},{9,8},{10,11... | collective-permute-start | bytes 3145736 | tf_op jit(solution)/shard_map/ppermute | solution.py:521
  46.3 14.8 %collective-permute-start.10 = (bf16[256,1024]{1,0:T(8,128)(2,1)S(1)}, bf16[256,1024]{1,0:T(8,128)(2,1)S(1)}, u32[]{:S(2)}, u32[]{:S(2)}) collective-permute-start(bf16[256,1024]{1,0:T(8,128)(2,1)S(1)} %project.11.after), channel_id=1, source_target_pairs={{0,2},{1,3},{2,0},{3,1},{4,6},{5,7},{6,4},{7,5},{8,10},{9,11},{10,... | collective-permute-start | bytes 1572872 | tf_op jit(solution)/shard_map/ppermute | solution.py:504
  47.3 18.9 %collective-permute-start.11 = (bf16[128,1024]{1,0:T(8,128)(2,1)S(1)}, bf16[128,1024]{1,0:T(8,128)(2,1)S(1)}, u32[]{:S(2)}, u32[]{:S(2)}) collective-permute-start(bf16[128,1024]{1,0:T(8,128)(2,1)S(1)} %project.12.after), channel_id=1, source_target_pairs={{0,2},{1,3},{2,0},{3,1},{4,6},{5,7},{6,4},{7,5},{8,10},{9,11},{10,... | collective-permute-start | bytes 786440 | tf_op jit(solution)/shard_map/ppermute | solution.py:504
